TPU v7x, 256 devices: a whole 4x4x8 slice. The times are simulated.
256 devices in a mesh: dp: 32 (over z_lo, x, core), group: 8 (over y, z_hi).
Axes of the slice: x: 4, y: 4, z: 8 (z_hi: 2, z_lo: 4; z = z_hi * 4 + z_lo), core: 2. Of those that a mesh axis runs over, the one named last changes fastest.
Arguments:
- cotangent: bfloat16 [32768, 2048], P(('dp', 'group')), may hold values from -6 to 6
- gate_weights: bfloat16 [32768, 8], P(('dp', 'group')), may hold values from 0.019897461 to 0.5
- expert_ids: int32 [32768, 8], P(('dp', 'group')), may hold values from 0 to 63, all different within a row; in each aligned block of 128 rows (0 to 127, 128 to 255, ...) at most 20 rows name the same one
- saved_hidden: bfloat16 [64, 5120, 768], P('dp', 'group'), may hold values from -6 to 6
- base_down: bfloat16 [64, 768, 2048], P('dp'), may hold values from -0.0029296875 to 0.0029296875
- factor_in: float32 [64, 64, 768], P('dp', 'group'), may hold values from -0.09375 to 0.09375
- factor_out: float32 [64, 64, 2048], P('dp', 'group'), may hold values from -0.09375 to 0.09375
- mean_in: float32 [64, 64, 768], P('dp', 'group'), may hold values from -0.625 to 0.625
- mean_out: float32 [64, 64, 2048], P('dp', 'group'), may hold values from -0.375 to 0.375
- square_in: float32 [64, 64, 768], P('dp', 'group'), may hold values from 2.260992e-05 to 0.00011442586
- square_out: float32 [64, 64, 2048], P('dp', 'group'), may hold values from 8.47872e-06 to 4.2909694e-05
- decode_hidden: bfloat16 [2, 64, 1024, 768], P(None, 'dp', 'group'), may hold values from -6 to 6
- decode_ids: int32 [2, 4096, 8], P(None, ('dp', 'group')), may hold values from 0 to 63, all different within a row; in each aligned block of 16 rows (0 to 15, 16 to 31, ..., all dimensions but the last counted through in order) at most 4 rows name the same one
- decode_gates: float32 [2, 4096, 8], P(None, ('dp', 'group')), may hold values from 0.02 to 0.5
- residual_in: bfloat16 [2, 4096, 2048], P(None, ('dp', 'group')), may hold values from -0.0625 to 0.0625
Outputs:
- hidden_grad: bfloat16 [64, 5120, 768], P('dp', 'group')
- adapted_in: float32 [64, 64, 768], P('dp', 'group')
- averaged_in: float32 [64, 64, 768], P('dp', 'group')
- squared_in: float32 [64, 64, 768], P('dp', 'group')
- adapted_out: float32 [64, 64, 2048], P('dp', 'group')
- averaged_out: float32 [64, 64, 2048], P('dp', 'group')
- squared_out: float32 [64, 64, 2048], P('dp', 'group')
- residual_out: bfloat16 [2, 4096, 2048], P(None, ('dp', 'group'))
Inputs may be any that keep to these rules, and one draw needn't show every extreme that they name: `expert_ids`: each row names 8 different experts. In each aligned block of 128 rows (the rows of one device) no expert is named by more than 20 rows, and in some block one expert is named by exactly 20 rows. `decode_ids`: each row names 8 different experts. Taking both leading dimensions in order, in each aligned block of 16 rows no expert is named by more than 4 rows, and in some block one expert is named by exactly 4 rows.
All inputs are finite; a program needn't handle non-finite values.
Results may differ from a plain program's by a relative error of at most 0.022.
Values may be sent and summed in bfloat16 or wider, within the bound.
A program may use at most 128 MiB of HBM per device.

v0:
```python
import jax
import jax.numpy as jnp
from jax import lax
from jax.sharding import PartitionSpec as P

delta_scale = 0.5
learn_rate = 0.005
beta_first = 0.9
beta_second = 0.999
adam_count = 20.0
adam_eps = 1e-08


def block_ranks(flat_ids, expert_count):
    onehot = (flat_ids[..., None] == jnp.arange(expert_count, dtype=jnp.int32)).astype(jnp.int32)
    running = jnp.cumsum(onehot, axis=-2)
    return jnp.sum(running * onehot, axis=-1) - 1


def adam_update(parameter, moment_one, moment_two, gradient):
    first_new = beta_first * moment_one + (1.0 - beta_first) * gradient
    second_new = beta_second * moment_two + (1.0 - beta_second) * gradient * gradient
    fix_first = 1.0 - beta_first**adam_count
    fix_second = 1.0 - beta_second**adam_count
    update = first_new / fix_first / (jnp.sqrt(second_new / fix_second) + adam_eps)
    return (parameter - learn_rate * update, first_new, second_new)


def on_device(
    cotangent,
    gate_weights,
    expert_ids,
    saved_hidden,
    base_down,
    factor_in,
    factor_out,
    mean_in,
    mean_out,
    square_in,
    square_out,
    decode_hidden,
    decode_ids,
    decode_gates,
    residual_in,
):
    dp_count = lax.axis_size("dp")
    group_count = lax.axis_size("group")
    exp_dev = base_down.shape[0]
    dmodel = base_down.shape[2]
    experts = exp_dev * dp_count
    slot_rows = saved_hidden.shape[1]
    capacity = slot_rows // dp_count
    learner_in, learner_out = (
        lax.all_gather(factor_in.astype(jnp.bfloat16), "group", axis=1, tiled=True),
        lax.all_gather(factor_out.astype(jnp.bfloat16), "group", axis=1, tiled=True),
    )
    flat_ids = expert_ids.reshape(-1)
    slot_rank = block_ranks(flat_ids, experts)
    target = flat_ids % exp_dev * slot_rows + flat_ids // exp_dev * capacity + slot_rank
    scaled = (
        gate_weights.astype(jnp.float32)[:, :, None] * cotangent.astype(jnp.float32)[:, None, :]
    ).astype(jnp.bfloat16)
    outgoing = (
        jnp.zeros((exp_dev * slot_rows, dmodel), jnp.bfloat16)
        .at[target]
        .set(scaled.reshape(-1, dmodel))
    )
    incoming = lax.all_to_all(
        outgoing.reshape(exp_dev, slot_rows, dmodel), "dp", split_axis=1, concat_axis=1, tiled=True
    )
    low_in = jnp.einsum(
        "emf,erf->emr", saved_hidden, learner_in, preferred_element_type=jnp.float32
    ).astype(jnp.bfloat16)
    low_out = jnp.einsum(
        "emd,erd->emr", incoming, learner_out, preferred_element_type=jnp.float32
    ).astype(jnp.bfloat16)
    base_part = jnp.einsum("emd,efd->emf", incoming, base_down, preferred_element_type=jnp.float32)
    side_part = jnp.einsum("emr,erf->emf", low_out, learner_in, preferred_element_type=jnp.float32)
    hidden_grad = (base_part + delta_scale * side_part).astype(jnp.bfloat16)
    share = delta_scale / group_count
    term_in = share * jnp.einsum(
        "emr,emf->erf", low_out, saved_hidden, preferred_element_type=jnp.float32
    )
    term_out = share * jnp.einsum(
        "emr,emd->erd", low_in, incoming, preferred_element_type=jnp.float32
    )
    grad_in, grad_out = (
        lax.psum_scatter(
            term_in.astype(jnp.bfloat16), "group", scatter_dimension=1, tiled=True
        ).astype(jnp.float32),
        lax.psum_scatter(
            term_out.astype(jnp.bfloat16), "group", scatter_dimension=1, tiled=True
        ).astype(jnp.float32),
    )
    adapted_in, averaged_in, squared_in = adam_update(factor_in, mean_in, square_in, grad_in)
    adapted_out, averaged_out, squared_out = adam_update(factor_out, mean_out, square_out, grad_out)
    rollout_in, rollout_out = (
        lax.all_gather(adapted_in.astype(jnp.bfloat16), "group", axis=1, tiled=True),
        lax.all_gather(adapted_out.astype(jnp.bfloat16), "group", axis=1, tiled=True),
    )
    decode_slots = decode_hidden.shape[2]
    decode_cap = decode_slots // dp_count
    delta_full = jnp.einsum(
        "erf,erd->efd", rollout_in, rollout_out, preferred_element_type=jnp.float32
    )
    merged = (base_down.astype(jnp.float32) + delta_scale * delta_full).astype(jnp.bfloat16)
    produced = jnp.einsum(
        "semf,efd->semd", decode_hidden, merged, preferred_element_type=jnp.float32
    ).astype(jnp.bfloat16)
    returned = lax.all_to_all(produced, "dp", split_axis=2, concat_axis=2, tiled=True)
    step_count = decode_ids.shape[0]
    rows_dev = decode_ids.shape[1]
    choose_total = decode_ids.shape[2]
    decode_flat = decode_ids.reshape(step_count, rows_dev * choose_total)
    decode_rank = block_ranks(decode_flat, experts)
    lookup = (
        decode_flat % exp_dev * decode_slots + decode_flat // exp_dev * decode_cap + decode_rank
    )
    flat_table = returned.reshape(step_count, exp_dev * decode_slots, dmodel)
    gathered = jax.vmap(lambda table_rows, index_rows: table_rows[index_rows])(flat_table, lookup)
    gathered = gathered.reshape(step_count, rows_dev, choose_total, dmodel).astype(jnp.float32)
    combined = jnp.sum(decode_gates[..., None] * gathered, axis=2)
    residual_out = (residual_in.astype(jnp.float32) + combined).astype(jnp.bfloat16)
    return (
        hidden_grad,
        adapted_in,
        averaged_in,
        squared_in,
        adapted_out,
        averaged_out,
        squared_out,
        residual_out,
    )


def solution(mesh):
    in_specs = (
        P(("dp", "group"), None),
        P(("dp", "group"), None),
        P(("dp", "group"), None),
        P("dp", "group", None),
        P("dp", None, None),
        P("dp", "group", None),
        P("dp", "group", None),
        P("dp", "group", None),
        P("dp", "group", None),
        P("dp", "group", None),
        P("dp", "group", None),
        P(None, "dp", "group", None),
        P(None, ("dp", "group"), None),
        P(None, ("dp", "group"), None),
        P(None, ("dp", "group"), None),
    )
    out_specs = (
        P("dp", "group", None),
        P("dp", "group", None),
        P("dp", "group", None),
        P("dp", "group", None),
        P("dp", "group", None),
        P("dp", "group", None),
        P("dp", "group", None),
        P(None, ("dp", "group"), None),
    )
    return jax.shard_map(
        on_device, mesh=mesh, in_specs=in_specs, out_specs=out_specs, check_vma=False
    )
```

profile of v0, /device:TPU:1, one launch (start us, length us, event | category | flops | bytes accessed | tf_op | source)
XLA Modules:
  0.0 546.8 jit_solution(16208123585650600754)
XLA Ops:
  7.2 0.9 copy.54
  8.4 18.0 %reduce-window.6 = s32[64,8,128]{2,1,0:T(8,128)S(1)} reduce-window(s32[64,8,128]{2,1,0:T(8,128)S(1)} %fusion.38, s32[]{:T(128)} %constant.48.clone.1), window={size=1x1x128 pad=0_0x0_0x127_0}, to_apply=%region_0.0 | reduce-window | flops 8323072 | bytes 524292 | tf_op jit(solution)/shard_map/reduce-window
  27.1 1.1 convert_element_type.74
  29.1 10.5 %scatter_custom_fusion = bf16[1280,2048]{1,0:T(8,128)(2,1)} fusion(s32[1024]{0:T(1024)S(1)} %bitcast.72, f32[128,2048]{1,0:T(8,128)S(1)} %convert_element_type.74, f32[1024]{0:T(1024)S(1)} %reshape.312, bf16[]{:T(256)} %constant.46.clone.1), kind=kCustom, calls=%fused_computation.9 | custom fusion | flops 4194304 | bytes 6295554 | tf_op jit(solution)/shard_map/scatter | solution.py:66
  39.6 10.2 %copy.60 = bf16[2,640,2048]{2,0,1:T(2,128)(2,1)} copy(bf16[2,640,2048]{2,1,0:T(8,128)(2,1)} %bitcast.62) | data formatting | bytes 10485760 | tf_op jit(solution)/shard_map/reshape | solution.py:69
  49.8 10.2 %all-to-all-start = ((bf16[2,640,2048]{2,0,1:T(2,128)(2,1)}), bf16[2,640,2048]{2,0,1:T(2,128)(2,1)}, u32[]{:S(2)}, u32[]{:S(2)}) async-start(bf16[2,640,2048]{2,0,1:T(2,128)(2,1)} %copy.60), calls=%async_computation | async-start | bytes 10485760 | tf_op jit(solution)/shard_map/all_to_all | solution.py:68
  60.1 126.9 %all_gather.13 = bf16[2,64,768]{2,1,0:T(8,128)(2,1)S(1)} all-gather(bf16[2,8,768]{2,1,0:T(8,128)(2,1)S(1)} %convert_element_type.78), channel_id=1, replica_groups=mesh['dp'=32,'group'=8] {'group'}, dimensions={1}, use_global_device_ids=true | all-gather | bytes 221184 | tf_op jit(solution)/shard_map/all_gather | solution.py:54
  187.1 6.3 %fusion.27 = bf16[2,64,2048]{2,1,0:T(8,128)(2,1)S(1)} fusion(bf16[2,640,2048]{2,0,1:T(2,128)(2,1)} %all-to-all-done, bf16[2,640,768]{2,1,0:T(8,128)(2,1)S(1)} %copy-done, bf16[2,64,768]{2,1,0:T(8,128)(2,1)S(1)} %all_gather.13), kind=kOutput, calls=%fused_computation.23 | convolution fusion | flops 461979648 | bytes 7929856 | tf_op jit(solution)/shard_map/emr,emd->erd/dot_general | solution.py:84
  193.9 1.0 copy.80
  194.9 83.4 %reduce-scatter.9.cloned.1.call-done = bf16[8,4096]{1,0:T(8,128)(2,1)} async-done(((bf16[64,4096]{1,0:T(8,128)(2,1)}), bf16[8,4096]{1,0:T(8,128)(2,1)}) %reduce-scatter.9.cloned.1.call-update) | async-done | bytes 65552
  280.1 42.2 %all_gather.12 = bf16[2,64,2048]{2,1,0:T(8,128)(2,1)S(1)} all-gather(bf16[2,8,2048]{2,1,0:T(8,128)(2,1)S(1)} %get-tuple-element.16), channel_id=1, replica_groups=mesh['dp'=32,'group'=8] {'group'}, dimensions={1}, use_global_device_ids=true | all-gather | bytes 589824 | tf_op jit(solution)/shard_map/all_gather | solution.py:55
  322.3 5.6 %fusion.32 = bf16[2,640,64]{1,2,0:T(8,128)(2,1)S(1)} fusion(bf16[2,64,2048]{2,1,0:T(8,128)(2,1)S(1)} %all_gather.12, bf16[2,640,2048]{2,0,1:T(2,128)(2,1)} %all-to-all-done), kind=kOutput, calls=%fused_computation.29 | convolution fusion | flops 335626240 | bytes 5931008 | tf_op jit(solution)/shard_map/emd,erd->emr/dot_general | solution.py:74
  329.2 45.5 %all_gather.15 = bf16[2,64,2048]{2,1,0:T(8,128)(2,1)S(1)} all-gather(bf16[2,8,2048]{2,1,0:T(8,128)(2,1)S(1)} %get-tuple-element.8), channel_id=1, replica_groups=mesh['dp'=32,'group'=8] {'group'}, dimensions={1}, use_global_device_ids=true | all-gather | bytes 589824 | tf_op jit(solution)/shard_map/all_gather | solution.py:99
  374.7 38.6 %reduce-scatter.7.cloned.1.call-done = bf16[8,1536]{1,0:T(8,128)(2,1)} async-done(((bf16[64,1536]{1,0:T(8,128)(2,1)}), bf16[8,1536]{1,0:T(8,128)(2,1)}) %reduce-scatter.7.cloned.1.call-update) | async-done | bytes 24592
  414.7 38.6 %all_gather.14 = bf16[2,64,768]{2,1,0:T(8,128)(2,1)S(1)} all-gather(bf16[2,8,768]{2,1,0:T(8,128)(2,1)S(1)} %get-tuple-element.12), channel_id=1, replica_groups=mesh['dp'=32,'group'=8] {'group'}, dimensions={1}, use_global_device_ids=true | all-gather | bytes 221184 | tf_op jit(solution)/shard_map/all_gather | solution.py:98
  453.3 8.2 %fusion.20 = bf16[2,2,128,2048]{2,3,0,1:T(8,128)(2,1)} fusion(bf16[2,768,2048]{2,1,0:T(8,128)(2,1)} %param.19, bf16[2,64,768]{2,1,0:T(8,128)(2,1)S(1)} %all_gather.14, bf16[2,64,2048]{2,1,0:T(8,128)(2,1)S(1)} %all_gather.15, bf16[2,2,128,768]{3,2,1,0:T(8,128)(2,1)} %param.26), kind=kOutput, calls=%fused_computation.20 | convolution fusion | flops 2026897408 | bytes 9895936 | tf_op jit(solution)/shard_map/semf,efd->semd/dot_general | solution.py:107
  461.5 6.3 %copy.67 = bf16[2,2,128,2048]{3,0,1,2:T(2,128)(2,1)} copy(bf16[2,2,128,2048]{2,3,0,1:T(8,128)(2,1)} %fusion.20) | data formatting | bytes 4194304 | tf_op jit(solution)/shard_map/convert_element_type | solution.py:109
  467.8 14.0 %all-to-all-start.1 = ((bf16[2,2,128,2048]{3,0,1,2:T(2,128)(2,1)}), bf16[2,2,128,2048]{3,0,1,2:T(2,128)(2,1)}, u32[]{:S(2)}, u32[]{:S(2)}) async-start(bf16[2,2,128,2048]{3,0,1,2:T(2,128)(2,1)} %copy.67), calls=%async_computation.1 | async-start | bytes 4194304 | tf_op jit(solution)/shard_map/all_to_all | solution.py:110
  482.6 10.6 %fusion.15 = f32[2,640,768]{2,1,0:T(8,128)S(1)} fusion(bf16[2,768,2048]{2,1,0:T(8,128)(2,1)} %param.19, bf16[2,640,2048]{2,0,1:T(2,128)(2,1)} %all-to-all-done), kind=kOutput, calls=%fused_computation.16 | convolution fusion | flops 4026531840 | bytes 15466496 | tf_op jit(solution)/shard_map/emd,efd->emf/dot_general | solution.py:77
  493.3 2.0 add_convert_fusion.1
  495.3 34.5 %all-to-all-done.1 = bf16[2,2,128,2048]{3,0,1,2:T(2,128)(2,1)} async-done(((bf16[2,2,128,2048]{3,0,1,2:T(2,128)(2,1)}), bf16[2,2,128,2048]{3,0,1,2:T(2,128)(2,1)}, u32[]{:S(2)}, u32[]{:S(2)}) %all-to-all-start.1) | async-done | bytes 2097184 | tf_op jit(solution)/shard_map/all_to_all | solution.py:110
  529.8 4.1 copy.68
  533.9 4.2 gather_fusion
  538.0 1.0 fusion.30
  (58 shorter events, 8.5 us)
Async XLA Ops:
  7.2 179.9 %copy-start = (bf16[2,640,768]{2,1,0:T(8,128)(2,1)S(1)}, bf16[2,640,768]{2,1,0:T(8,128)(2,1)}, u32[]{:S(2)}) copy-start(bf16[2,640,768]{2,1,0:T(8,128)(2,1)} %param.18) | copy-start | bytes 5898244
  49.8 10.3 %copy-start.1 = (f32[2,8,768]{2,1,0:T(8,128)S(1)}, f32[2,8,768]{2,1,0:T(8,128)}, u32[]{:S(2)}) copy-start(f32[2,8,768]{2,1,0:T(8,128)} %param.20) | copy-start | bytes 147460
  49.8 137.2 %all-to-all-start = ((bf16[2,640,2048]{2,0,1:T(2,128)(2,1)}), bf16[2,640,2048]{2,0,1:T(2,128)(2,1)}, u32[]{:S(2)}, u32[]{:S(2)}) async-start(bf16[2,640,2048]{2,0,1:T(2,128)(2,1)} %copy.60), calls=%async_computation | async-start | bytes 10485760 | tf_op jit(solution)/shard_map/all_to_all | solution.py:68
  60.0 218.3 %reduce-scatter.9.cloned.1.call-start = ((), (), s32[]{:S(2)}) async-start(), calls=%async_computation.5 | async-start | bytes 589824
  187.0 92.2 %copy-start.2 = (f32[2,8,2048]{2,1,0:T(8,128)S(1)}, f32[2,8,2048]{2,1,0:T(8,128)}, u32[]{:S(2)}) copy-start(f32[2,8,2048]{2,1,0:T(8,128)} %param.21) | copy-start | bytes 393220
  187.1 92.2 %copy-start.3 = (f32[2,8,2048]{2,1,0:T(8,128)S(1)}, f32[2,8,2048]{2,1,0:T(8,128)}, u32[]{:S(2)}) copy-start(f32[2,8,2048]{2,1,0:T(8,128)} %param.23) | copy-start | bytes 393220
  187.1 92.2 %copy-start.4 = (f32[2,8,2048]{2,1,0:T(8,128)S(1)}, f32[2,8,2048]{2,1,0:T(8,128)}, u32[]{:S(2)}) copy-start(f32[2,8,2048]{2,1,0:T(8,128)} %param.25) | copy-start | bytes 393220
  194.9 218.4 %reduce-scatter.7.cloned.1.call-start = ((), (), s32[]{:S(2)}) async-start(), calls=%async_computation.4 | async-start | bytes 221184
  322.3 91.8 %copy-start.6 = (f32[2,8,768]{2,1,0:T(8,128)S(1)}, f32[2,8,768]{2,1,0:T(8,128)}, u32[]{:S(2)}) copy-start(f32[2,8,768]{2,1,0:T(8,128)} %param.22) | copy-start | bytes 147460
  322.3 91.8 %copy-start.7 = (f32[2,8,768]{2,1,0:T(8,128)S(1)}, f32[2,8,768]{2,1,0:T(8,128)}, u32[]{:S(2)}) copy-start(f32[2,8,768]{2,1,0:T(8,128)} %param.24) | copy-start | bytes 147460
  461.5 20.3 %copy-start.8 = (s32[2,16,8]{1,2,0:T(8,128)S(1)}, s32[2,16,8]{1,2,0:T(8,128)}, u32[]{:S(2)}) copy-start(s32[2,16,8]{1,2,0:T(8,128)} %param.27) | copy-start | bytes 3076
  461.5 20.9 %copy-start.9 = (f32[2,16,8]{1,2,0:T(8,128)S(1)}, f32[2,16,8]{1,2,0:T(8,128)}, u32[]{:S(2)}) copy-start(f32[2,16,8]{1,2,0:T(8,128)} %param.28) | copy-start | bytes 3076
  467.8 62.0 %all-to-all-start.1 = ((bf16[2,2,128,2048]{3,0,1,2:T(2,128)(2,1)}), bf16[2,2,128,2048]{3,0,1,2:T(2,128)(2,1)}, u32[]{:S(2)}, u32[]{:S(2)}) async-start(bf16[2,2,128,2048]{3,0,1,2:T(2,128)(2,1)} %copy.67), calls=%async_computation.1 | async-start | bytes 4194304 | tf_op jit(solution)/shard_map/all_to_all | solution.py:110
  533.9 5.2 copy-start.5
Sparse Core Ops, SparseCore 0:
  195.0 83.3 reduce-scatter.8
  329.4 83.8 reduce-scatter.6
where the time goes:
time: 553 us; the launch traced here: 547 us
  blocking collectives  253 us (46%)
  waiting for transfers between devices  157 us (28%)
  other arithmetic  33.6 us (6%)
  matrix products  33.1 us (6%)
  local copies, waits for them, and re-layouts  31.6 us (6%)
  starting transfers between devices  24.3 us (4%)
  between operations  14.5 us (3%)
    all_gather x1, blocking collectives, on_device(): lax.all_gather(factor_in.astype(jnp.bfloat16), 'group', axis=1, tiled=True)  127 us
    unnamed x4, waiting for transfers between devices  122 us
    all_gather x1, blocking collectives, on_device(): lax.all_gather(adapted_out.astype(jnp.bfloat16), 'group', axis=1, tiled=T...  45.5 us
    all_gather x1, blocking collectives, on_device(): lax.all_gather(factor_out.astype(jnp.bfloat16), 'group', axis=1, tiled=True)  42.2 us
    all_gather x1, blocking collectives, on_device(): lax.all_gather(adapted_in.astype(jnp.bfloat16), 'group', axis=1, tiled=True)  38.6 us
    all_to_all x1, waiting for transfers between devices, on_device(): lax.all_to_all(produced, 'dp', split_axis=2, concat_axis=2, tiled=True)  34.5 us
    another operation x3, other arithmetic  18.2 us
    all_to_all x1, starting transfers between devices, on_device(): lax.all_to_all(produced, 'dp', split_axis=2, concat_axis=2, tiled=True)  14 us
  transfers between devices with their start and end apart: 4, of which 3 were waited for; matrix products, arithmetic and copies ran while one was open for 2% of the time, Pallas kernels for 0%

commit v1 on v0

v1 whole, which is shorter than its diff:
```python
import functools

import jax
import jax.numpy as jnp
from jax import lax
from jax.experimental import pallas as pl
from jax.experimental.pallas import tpu as pltpu
from jax.sharding import PartitionSpec as P

delta_scale = 0.5
learn_rate = 0.005
beta_first = 0.9
beta_second = 0.999
adam_count = 20.0
adam_eps = 1e-08

BF = jnp.bfloat16
F32 = jnp.float32
MESH = pl.DeviceIdType.MESH

NZ, NX, NC = 4, 4, 2
NQ = NX * NC
NY, NH = 4, 2
D, FF, CAP, CAPD = 2048, 768, 20, 4
TOK, DEC = 128, 32
NCH = 4
CW = D // NCH
SB = NZ * CAP
DB = NZ * 2 * CAPD
PIECES = ((0, 512), (512, 512), (1024, 512), (1536, 1280))
W = D + FF


def nt(a, b):
    return lax.dot_general(a, b, (((1,), (1,)), ((), ())), preferred_element_type=F32)


def tn(a, b):
    return lax.dot_general(a, b, (((0,), (0,)), ((), ())), preferred_element_type=F32)


def mm(a, b):
    return jnp.dot(a, b, preferred_element_type=F32)


def iota(shape, axis):
    return lax.broadcasted_iota(jnp.int32, shape, axis)


def adam_update(parameter, moment_one, moment_two, gradient):
    first_new = beta_first * moment_one + (1.0 - beta_first) * gradient
    second_new = beta_second * moment_two + (1.0 - beta_second) * gradient * gradient
    fix_first = 1.0 - beta_first**adam_count
    fix_second = 1.0 - beta_second**adam_count
    update = first_new / fix_first / (jnp.sqrt(second_new / fix_second) + adam_eps)
    return (parameter - learn_rate * update, first_new, second_new)


def kernel(
    ids_ref, gates_ref, dids_ref, dgates_ref, fin_ref, fout_ref,
    cot_hbm, saved_hbm, base_hbm, min_hbm, mout_hbm, sin_hbm, sout_hbm, dh_hbm, res_hbm,
    hg_hbm, ain_ref, vin_ref, qin_ref, aout_ref, vout_ref, qout_ref, rout_ref,
    xa, lms, lmr, dms, dmr, fg, pmat, lr, lg, ob, inc,
    saved, base, mi, mo, si, so, dh, res,
    perm, savedp, lit, lo, tg, ry, ss, sz, rz, rg,
    hgacc, hgp, hgn, dperm, dhp, dbase, amat, drs, pd, rd, pz, rzd,
    in_sem, out_sem, zt_s, zt_r, lm_s, lm_r, dm_s, dm_r, fz_s, fz_r, fy_s, fy_r,
    x_s, x_r, ry_s, ry_r, rz_s, rz_r, az_s, az_r, ay_s, ay_r, dx_s, dx_r, dz_s, dz_r,
):
    dp = lax.axis_index("dp")
    grp = lax.axis_index("group")
    z = dp // NQ
    q = dp % NQ
    x = q // NC
    c = q % NC
    y = grp // NH
    h = grp % NH

    def zdev(z2):
        return (z2 * NQ + q, grp)

    def qdev(q2):
        return (z * NQ + q2, grp)

    def ydev(y2):
        return (dp, y2 * NH + h)

    hdev = (dp, y * NH + (1 - h))
    zpeers = [(z + k) % NZ for k in (1, 2, 3)]
    ypeers = [(y + k) % NY for k in (2, 1, 3)]
    qpeers = [
        ((x + dx) % NX) * NC + (c + dc) % NC
        for dx, dc in ((2, 0), (2, 1), (1, 0), (3, 1), (1, 1), (3, 0), (0, 1))
    ]
    sends = []

    def push(src, dst, ssem, rsem, dev):
        cp = pltpu.make_async_remote_copy(
            src_ref=src, dst_ref=dst, send_sem=ssem, recv_sem=rsem, device_id=dev, device_id_type=MESH
        )
        cp.start()
        sends.append(cp)

    def arrived(dst, ssem, rsem, dev):
        pltpu.make_async_remote_copy(
            src_ref=dst, dst_ref=dst, send_sem=ssem, recv_sem=rsem, device_id=dev, device_id_type=MESH
        ).wait_recv()

    loads = {}

    def load(name, k, src, dst):
        cp = pltpu.make_async_copy(src, dst, in_sem.at[k])
        cp.start()
        loads[name] = cp

    own_rows = pl.ds(pl.multiple_of(z * TOK, TOK), TOK)
    for ch in range(NCH):
        load(("cot", ch), ch, cot_hbm.at[:, pl.ds(ch * CW, CW)], xa.at[ch, own_rows])
    load("saved", 4, saved_hbm, saved)
    load("base", 5, base_hbm, base)
    load("dh", 6, dh_hbm, dh)
    load("mi", 7, min_hbm, mi)
    load("mo", 8, mout_hbm, mo)
    load("si", 9, sin_hbm, si)
    load("so", 10, sout_hbm, so)
    load("res", 11, res_hbm, res)

    barrier = pltpu.get_barrier_semaphore()
    for z2 in zpeers:
        pl.semaphore_signal(barrier, inc=1, device_id=zdev(z2), device_id_type=MESH)
    for q2 in qpeers:
        pl.semaphore_signal(barrier, inc=1, device_id=qdev(q2), device_id_type=MESH)
    for y2 in ypeers:
        pl.semaphore_signal(barrier, inc=1, device_id=ydev(y2), device_id_type=MESH)
    pl.semaphore_signal(barrier, inc=1, device_id=hdev, device_id_type=MESH)

    own = pl.ds(grp, 1)
    fg[own, :, 0:D] = fout_ref[...].astype(BF)[None]
    fg[own, :, D:W] = fin_ref[...].astype(BF)[None]

    lane = iota((TOK, 128), 1)
    count = jnp.zeros((TOK, 128), F32)
    gate = jnp.zeros((TOK, 128), F32)
    ids = ids_ref[...]
    gw = gates_ref[...].astype(F32)
    for k in range(8):
        hit = ids[:, k : k + 1] == lane
        count = count + jnp.where(hit, 1.0, 0.0)
        gate = gate + jnp.where(hit, gw[:, k : k + 1], 0.0)
    rows, cols = iota((TOK, TOK), 0), iota((TOK, TOK), 1)
    before = jnp.where(rows < cols, 1.0, 0.0).astype(BF)
    eye = jnp.where(rows == cols, 1.0, 0.0).astype(BF)
    cb = count.astype(BF)
    rank_t = tn(cb, before)
    count_t = tn(cb, eye)
    gate_t = tn(gate.astype(BF), eye)
    row_t = jnp.where(count_t > 0.5, rank_t + (CAP * z).astype(F32), -1.0).astype(BF)
    gate_t = gate_t.astype(BF)
    for z2 in range(NZ):
        lms[z2, 0:16] = row_t[16 * z2 : 16 * z2 + 16]
        lms[z2, 16:32] = gate_t[16 * z2 : 16 * z2 + 16]

    lane = iota((DEC, 128), 1)
    count = jnp.zeros((DEC, 128), F32)
    gate = jnp.zeros((DEC, 128), F32)
    ids = dids_ref[...]
    gw = dgates_ref[...]
    for k in range(8):
        hit = ids[:, k : k + 1] == lane
        count = count + jnp.where(hit, 1.0, 0.0)
        gate = gate + jnp.where(hit, gw[:, k : k + 1], 0.0)
    rows, cols = iota((DEC, DEC), 0), iota((DEC, DEC), 1)
    before = jnp.where((cols < rows) & ((cols >> 4) == (rows >> 4)), 1.0, 0.0).astype(BF)
    rank = mm(before, count.astype(BF))
    high = gate.astype(BF)
    dms[0:32] = jnp.where(count > 0.5, rank, -1.0).astype(BF)
    dms[32:64] = high
    dms[64:96] = (gate - high.astype(F32)).astype(BF)

    pl.semaphore_wait(barrier, 14)

    push(fg.at[own], fg.at[own], fz_s.at[0], fz_r.at[0], hdev)
    for k, z2 in enumerate(zpeers):
        push(lms.at[z2], lmr.at[z], lm_s.at[k], lm_r.at[z], zdev(z2))

    def send_tokens(ch):
        loads[("cot", ch)].wait()
        for k, z2 in enumerate(zpeers):
            push(xa.at[ch, own_rows], xa.at[ch, own_rows], zt_s.at[ch, k], zt_r.at[ch, z], zdev(z2))

    send_tokens(0)
    send_tokens(1)
    for k, z2 in enumerate(zpeers):
        push(dms, dmr.at[z], dm_s.at[k], dm_r.at[z], zdev(z2))
    lmr[pl.ds(z, 1)] = lms[pl.ds(z, 1)]
    dmr[pl.ds(z, 1)] = dms[...][None]

    pair = pl.ds(pl.multiple_of(y * NH, NH), NH)
    other = pl.ds(y * NH + (1 - h), 1)
    arrived(fg.at[other], fz_s.at[0], fz_r.at[0], hdev)
    for k, y2 in enumerate(ypeers):
        push(fg.at[pair], fg.at[pair], fy_s.at[k], fy_r.at[y], ydev(y2))

    for z2 in zpeers:
        arrived(lmr.at[z2], lm_s.at[0], lm_r.at[z2], zdev(z2))
    for z2 in range(NZ):
        lr[:, z2 * TOK : (z2 + 1) * TOK] = lmr[z2, 0:16].astype(F32)
        lg[:, z2 * TOK : (z2 + 1) * TOK] = lmr[z2, 16:32].astype(F32)
    slot = iota((SB, NZ * TOK), 0).astype(F32)

    def build_p(e, carry):
        row = lr[pl.ds(e, 1), :]
        val = lg[pl.ds(e, 1), :]
        pmat[e] = jnp.where(slot == row, val, 0.0).astype(BF)
        return carry

    lax.fori_loop(0, 2 * NQ, build_p, 0)

    def expand(ch, q2):
        w = pmat[pl.ds(q2 * 2, 2)].reshape(2 * SB, NZ * TOK)
        return mm(w, xa[ch]).astype(BF).reshape(2, SB, CW)

    def build_send(ch):
        for z2 in zpeers:
            dst = xa.at[ch, pl.ds(pl.multiple_of(z2 * TOK, TOK), TOK)]
            arrived(dst, zt_s.at[ch, 0], zt_r.at[ch, z2], zdev(z2))
        if ch + 2 < NCH:
            send_tokens(ch + 2)
        for k, q2 in enumerate(qpeers):
            ob[ch, k] = expand(ch, q2)
            push(ob.at[ch, k], inc.at[ch, :, q], x_s.at[ch, k], x_r.at[ch, q], qdev(q2))
        inc[ch, :, pl.ds(q, 1)] = expand(ch, q)[:, None]

    build_send(0)

    def permutation(n, source):
        return jnp.where(iota((n, n), 1) == source, 1.0, 0.0).astype(BF)

    p_id = iota((NQ * SB, NQ * SB), 0)
    blk = (p_id * 3277) >> 16
    off = p_id - blk * CAP
    perm[0] = permutation(NQ * SB, (blk & 3) * (NQ * CAP) + (blk >> 2) * CAP + off)
    perm[1] = permutation(NQ * SB, (blk & 7) * SB + (blk >> 3) * CAP + off)
    loads["saved"].wait()

    def permute_saved(e, carry):
        savedp[e] = mm(perm[0], saved[e]).astype(BF)
        return carry

    lax.fori_loop(0, 2, permute_saved, 0)

    for y2 in ypeers:
        blocks = pl.ds(pl.multiple_of(y2 * NH, NH), NH)
        arrived(fg.at[blocks], fy_s.at[0], fy_r.at[y2], ydev(y2))

    def lane_mask(n, e):
        return ((iota((n, 128), 1) >> 3) & 1) == e

    def low_in(e, carry):
        low = nt(savedp[e], fg[:, :, D:W].reshape(128, FF))
        low = jnp.where(lane_mask(NQ * SB, e), low, 0.0)
        lit[e] = low.T.astype(BF)
        lo[e] = jnp.zeros((NQ * SB, 128), F32)
        return carry

    lax.fori_loop(0, 2, low_in, 0)

    build_send(1)

    def consume(ch):
        for q2 in qpeers:
            arrived(inc.at[ch, :, q2], x_s.at[ch, 0], x_r.at[ch, q2], qdev(q2))
        cc = pl.ds(ch * CW, CW)
        weights = fg[:, :, cc].reshape(128, CW)

        def one(e, acc):
            rows = inc[ch, e].reshape(NQ * SB, CW)
            lo[e] += nt(rows, weights)
            return acc + mm(lit[e], rows)

        term = lax.fori_loop(0, 2, one, jnp.zeros((128, CW), F32))
        tg[:, :, cc] = term.astype(BF).reshape(8, 16, CW)

    def cols_of(p):
        return pl.ds(PIECES[p][0], PIECES[p][1])

    def rs_start(p):
        cc = cols_of(p)
        for k, y2 in enumerate(ypeers):
            src = tg.at[pl.ds(pl.multiple_of(y2 * NH, NH), NH), :, cc]
            push(src, ry.at[y, :, :, cc], ry_s.at[p, k], ry_r.at[p, y], ydev(y2))
        ry[pl.ds(y, 1), :, :, cc] = tg[pair, :, cc][None]

    def rs_mid(p):
        cc = cols_of(p)
        for y2 in ypeers:
            arrived(ry.at[y2, :, :, cc], ry_s.at[p, 0], ry_r.at[p, y2], ydev(y2))
        total = ry[0, :, :, cc].astype(F32)
        for y2 in range(1, NY):
            total = total + ry[y2, :, :, cc].astype(F32)
        ss[:, :, cc] = total
        sz[:, cc] = ss[1 - h, :, cc].astype(BF)
        push(sz.at[:, cc], rz.at[:, cc], rz_s.at[p], rz_r.at[p], hdev)

    def rs_fin(p):
        cc = cols_of(p)
        arrived(rz.at[:, cc], rz_s.at[p], rz_r.at[p], hdev)
        share = delta_scale / (NY * NH)

        def grad(start, width):
            at = pl.ds(start, width)
            return share * (ss[h, :, at] + rz[:, at].astype(F32))

        start = PIECES[p][0]
        at = pl.ds(start, CW)
        new, first, second = adam_update(fout_ref[:, at], mo[:, at], so[:, at], grad(start, CW))
        aout_ref[:, at], vout_ref[:, at], qout_ref[:, at] = new, first, second
        rg[own, :, at] = new.astype(BF)[None]
        if p == NCH - 1:
            new, first, second = adam_update(fin_ref[...], mi[...], si[...], grad(D, FF))
            ain_ref[...], vin_ref[...], qin_ref[...] = new, first, second
            rg[own, :, D:W] = new.astype(BF)[None]
        push(rg.at[own, :, cc], rg.at[own, :, cc], az_s.at[p], az_r.at[p], hdev)

    def ag_mid(p):
        cc = cols_of(p)
        arrived(rg.at[other, :, cc], az_s.at[p], az_r.at[p], hdev)
        for k, y2 in enumerate(ypeers):
            push(rg.at[pair, :, cc], rg.at[pair, :, cc], ay_s.at[p, k], ay_r.at[p, y], ydev(y2))

    def ag_fin(p):
        cc = cols_of(p)
        for y2 in ypeers:
            blocks = pl.ds(pl.multiple_of(y2 * NH, NH), NH)
            arrived(rg.at[blocks, :, cc], ay_s.at[p, 0], ay_r.at[p, y2], ydev(y2))

    n = iota((512, 512), 0)
    source = ((n >> 2) & 1) * 256 + (n >> 8) * 128 + ((n >> 3) & 3) * 32 + ((n >> 5) & 7) * 4 + (n & 3)
    dperm[...] = permutation(512, source)
    loads["dh"].wait()
    dhp[...] = mm(dperm[...], dh[...]).astype(BF).reshape(2, 256, FF)
    loads["base"].wait()

    def base_product(k, carry):
        e, ch = k // NCH, k % NCH
        at = pl.ds(pl.multiple_of(ch * CW, CW), CW)
        dbase[e, :, at] = mm(dhp[e], base[e, :, at])
        return carry

    lax.fori_loop(0, 2 * NCH, base_product, 0)

    consume(0)
    rs_start(0)
    build_send(2)

    for z2 in zpeers:
        arrived(dmr.at[z2], dm_s.at[0], dm_r.at[z2], zdev(z2))
    for z2 in range(NZ):
        for k in range(3):
            drs[k, z2 * DEC : (z2 + 1) * DEC] = dmr[z2, k * DEC : (k + 1) * DEC]
    j = iota((128, 512), 1)
    spread = jnp.where(iota((128, 512), 0) == z * 16 + (j >> 5), 1.0, 0.0).astype(BF)
    i = iota((128, 512), 0)
    ok = (mm(drs[0], spread) == (j & 3).astype(F32)) & ((i >> 5) == ((j >> 3) & 3)) & (((i >> 4) & 1) == ((j >> 2) & 1))
    amat[0] = jnp.where(ok, mm(drs[1], spread), 0.0).astype(BF)
    amat[1] = jnp.where(ok, mm(drs[2], spread), 0.0).astype(BF)

    for name in ("mi", "mo", "si", "so", "res"):
        loads[name].wait()

    consume(1)
    rs_start(1)
    rs_mid(0)
    build_send(3)
    consume(2)
    rs_start(2)
    rs_mid(1)
    rs_fin(0)
    consume(3)

    def term_in(e, acc):
        low = jnp.where(lane_mask(NQ * SB, e), lo[e], 0.0)
        lo[e] = low
        return acc + mm(low.T.astype(BF), savedp[e])

    term = lax.fori_loop(0, 2, term_in, jnp.zeros((128, FF), F32))
    tg[:, :, D:W] = term.astype(BF).reshape(8, 16, FF)
    rs_start(3)
    rs_mid(2)
    rs_fin(1)
    ag_mid(0)

    def hidden(e):
        hgacc[...] = delta_scale * mm(lo[e].astype(BF), fg[:, :, D:W].reshape(128, FF))

        def part(ch, carry):
            at = pl.ds(pl.multiple_of(ch * CW, CW), CW)
            hgacc[...] += nt(inc[ch, e].reshape(NQ * SB, CW), base[e, :, at])
            return carry

        lax.fori_loop(0, NCH, part, 0)
        hgp[...] = hgacc[...].astype(BF)
        hgn[e] = mm(perm[1], hgp[...]).astype(BF)
        cp = pltpu.make_async_copy(hgn.at[e], hg_hbm.at[e], out_sem.at[e])
        cp.start()
        return cp

    out0 = hidden(0)
    rs_mid(3)
    rs_fin(2)
    ag_mid(1)
    rs_fin(3)
    ag_mid(2)
    out1 = hidden(1)
    ag_mid(3)
    ag_fin(0)
    ag_fin(1)
    ag_fin(2)
    ag_fin(3)

    low_d = []
    for e in range(2):
        low = nt(dhp[e], rg[:, :, D:W].reshape(128, FF))
        low_d.append(jnp.where(lane_mask(256, e), low, 0.0).astype(BF))
    for ch in range(NCH):
        at = pl.ds(ch * CW, CW)
        weights = rg[:, :, at].reshape(128, CW)
        for e in range(2):
            made = dbase[e, :, at] + delta_scale * mm(low_d[e], weights)
            pd[ch, :, e] = made.astype(BF).reshape(NQ, DB, CW)
        for k, q2 in enumerate(qpeers):
            push(pd.at[ch, q2], rd.at[ch, q], dx_s.at[ch, k], dx_r.at[ch, q], qdev(q2))
        rd[ch, pl.ds(q, 1)] = pd[ch, pl.ds(q, 1)]
    for ch in range(NCH):
        for q2 in qpeers:
            arrived(rd.at[ch, q2], dx_s.at[ch, 0], dx_r.at[ch, q2], qdev(q2))
        rows = rd[ch].reshape(512, CW)
        part = mm(amat[0], rows) + mm(amat[1], rows)
        pz[ch] = part.astype(BF).reshape(NZ, DEC, CW)
        for k, z2 in enumerate(zpeers):
            push(pz.at[ch, z2], rzd.at[ch, z], dz_s.at[ch, k], dz_r.at[ch, z], zdev(z2))
        rzd[ch, pl.ds(z, 1)] = pz[ch, pl.ds(z, 1)]
    for ch in range(NCH):
        at = pl.ds(ch * CW, CW)
        for z2 in zpeers:
            arrived(rzd.at[ch, z2], dz_s.at[ch, 0], dz_r.at[ch, z2], zdev(z2))
        total = res[:, at].astype(F32)
        for z2 in range(NZ):
            total = total + rzd[ch, z2].astype(F32)
        rout_ref[:, at] = total.astype(BF)

    out0.wait()
    out1.wait()
    for cp in sends:
        cp.wait_send()


def on_device(
    cotangent, gate_weights, expert_ids, saved_hidden, base_down, factor_in, factor_out,
    mean_in, mean_out, square_in, square_out, decode_hidden, decode_ids, decode_gates, residual_in,
):
    flat = lambda a: a.reshape(16, a.shape[-1])
    vm = pl.BlockSpec(memory_space=pltpu.VMEM)
    hbm = pl.BlockSpec(memory_space=pl.ANY)
    sds = jax.ShapeDtypeStruct
    V = pltpu.VMEM
    S = pltpu.SemaphoreType.DMA
    n = NQ * SB
    scratch = [
        V((NCH, NZ * TOK, CW), BF),
        V((NZ, 32, TOK), BF), V((NZ, 32, TOK), BF), V((96, 128), BF), V((NZ, 96, 128), BF),
        V((8, 16, W), BF),
        V((2 * NQ, SB, NZ * TOK), BF), V((16, NZ * TOK), F32), V((16, NZ * TOK), F32),
        V((NCH, 7, 2, SB, CW), BF), V((NCH, 2, NQ, SB, CW), BF),
        V((2, n, FF), BF), V((2, FF, D), BF),
        V((16, FF), F32), V((16, D), F32), V((16, FF), F32), V((16, D), F32),
        V((512, FF), BF), V((DEC, D), BF),
        V((2, n, n), BF), V((2, n, FF), BF), V((2, 128, n), BF), V((2, n, 128), F32),
        V((8, 16, W), BF), V((NY, NH, 16, W), BF), V((NH, 16, W), F32),
        V((16, W), BF), V((16, W), BF), V((8, 16, W), BF),
        V((n, FF), F32), V((n, FF), BF), V((2, n, FF), BF),
        V((512, 512), BF), V((2, 256, FF), BF), V((2, 256, D), F32),
        V((2, 128, 512), BF), V((3, 128, 128), BF),
        V((NCH, NQ, 2, DB, CW), BF), V((NCH, NQ, 2, DB, CW), BF),
        V((NCH, NZ, DEC, CW), BF), V((NCH, NZ, DEC, CW), BF),
        S((12,)), S((2,)), S((NCH, 3)), S((NCH, NZ)), S((3,)), S((NZ,)), S((3,)), S((NZ,)),
        S((1,)), S((1,)), S((3,)), S((NY,)),
        S((NCH, 7)), S((NCH, NQ)), S((NCH, 3)), S((NCH, NY)), S((NCH,)), S((NCH,)),
        S((NCH,)), S((NCH,)), S((NCH, 3)), S((NCH, NY)),
        S((NCH, 7)), S((NCH, NQ)), S((NCH, 3)), S((NCH, NZ)),
    ]
    outs = pl.pallas_call(
        kernel,
        out_shape=(
            sds((2, n, FF), BF),
            sds((16, FF), F32), sds((16, FF), F32), sds((16, FF), F32),
            sds((16, D), F32), sds((16, D), F32), sds((16, D), F32),
            sds((DEC, D), BF),
        ),
        in_specs=[vm] * 6 + [hbm] * 9,
        out_specs=(hbm,) + (vm,) * 7,
        scratch_shapes=scratch,
        compiler_params=pltpu.CompilerParams(
            collective_id=0, has_side_effects=True, vmem_limit_bytes=60 * 1024 * 1024
        ),
    )(
        expert_ids, gate_weights, decode_ids.reshape(DEC, 8), decode_gates.reshape(DEC, 8),
        flat(factor_in), flat(factor_out),
        cotangent, saved_hidden, base_down, flat(mean_in), flat(mean_out), flat(square_in), flat(square_out),
        decode_hidden.reshape(512, FF), residual_in.reshape(DEC, D),
    )
    hg, ain, vin, qin, aout, vout, qout, rout = outs
    wide = lambda a: a.reshape(2, 8, a.shape[-1])
    return (
        hg, wide(ain), wide(vin), wide(qin), wide(aout), wide(vout), wide(qout),
        rout.reshape(2, DEC // 2, D),
    )


def solution(mesh):
    in_specs = (
        P(("dp", "group"), None),
        P(("dp", "group"), None),
        P(("dp", "group"), None),
        P("dp", "group", None),
        P("dp", None, None),
        P("dp", "group", None),
        P("dp", "group", None),
        P("dp", "group", None),
        P("dp", "group", None),
        P("dp", "group", None),
        P("dp", "group", None),
        P(None, "dp", "group", None),
        P(None, ("dp", "group"), None),
        P(None, ("dp", "group"), None),
        P(None, ("dp", "group"), None),
    )
    out_specs = (
        P("dp", "group", None),
        P("dp", "group", None),
        P("dp", "group", None),
        P("dp", "group", None),
        P("dp", "group", None),
        P("dp", "group", None),
        P("dp", "group", None),
        P(None, ("dp", "group"), None),
    )
    return jax.shard_map(
        on_device, mesh=mesh, in_specs=in_specs, out_specs=out_specs, check_vma=False
    )
```

time: 553 us -> 159 us (0.29); the launches traced: 547 us -> 158 us
  blocking collectives: 253 us -> 0 us
  waiting for transfers between devices: 157 us -> 0 us
  Pallas kernels: 0 us -> 145 us
  other arithmetic: 33.6 us -> 0 us
  matrix products: 33.1 us -> 0 us
  starting transfers between devices: 24.3 us -> 0 us
  local copies, waits for them, and re-layouts: 31.6 us -> 13.1 us
  between operations: 14.5 us -> 0.71 us
    all_gather x4 -> x0, blocking collectives: 253 us -> none  [the longest x1 127 us: on_device(): lax.all_gather(factor_in.astype(jnp.bfloat16), 'group', axis=1, tiled=True)]
    pallas_call x0 -> x1, Pallas kernels: none -> 145 us  [on_device(): pl.pallas_call(kernel, out_shape=(sds((2, n, FF), BF), sds((16, FF), F32)...]
    unnamed x4 -> x0, waiting for transfers between devices: 122 us -> none
    all_to_all x2 -> x0, waiting for transfers between devices: 34.5 us -> none  [the longest x1 34.5 us: on_device(): lax.all_to_all(produced, 'dp', split_axis=2, concat_axis=2, tiled=True)]
    dot_general x6 -> x0, matrix products: 33.1 us -> none  [the longest x1 10.6 us: on_device(): jnp.einsum('emd,efd->emf', incoming, base_down, preferred_element_type=jn...]
    all_to_all x2 -> x0, starting transfers between devices: 24.2 us -> none  [the longest x1 14 us: on_device(): lax.all_to_all(produced, 'dp', split_axis=2, concat_axis=2, tiled=True)]
    another operation x4 -> x0, other arithmetic: 18.4 us -> none
    scatter x1 -> x0, other arithmetic: 10.5 us -> none  [on_device(): outgoing = jnp.zeros((exp_dev * slot_rows, dmodel), jnp.bfloat16).at[targ...]
  transfers between devices with their start and end apart: 4 -> 0, of which waited for: 3 -> 0; matrix products, arithmetic and copies ran while one was open for 2% -> 0% of each run, Pallas kernels for 0% -> 0%
where the time goes in v1:
time: 159 us; the launch traced here: 158 us
  Pallas kernels  145 us (91%)
  local copies, waits for them, and re-layouts  13.1 us (8%)
    pallas_call x1, Pallas kernels, on_device(): pl.pallas_call(kernel, out_shape=(sds((2, n, FF), BF), sds((16, FF), F32)...  145 us
    unnamed x26, local copies, waits for them, and re-layouts  13.1 us

profile of v1, /device:TPU:1, one launch (start us, length us, event | category | flops | bytes accessed | tf_op | source)
XLA Modules:
  0.0 158.5 jit_solution(11649198973025723813)
XLA Ops:
  0.6 1.4 copy.23
  2.0 1.4 copy.24
  3.4 1.4 copy.26.gates_ref
  4.8 1.4 copy.25.ids_ref
  6.2 144.7 %shard_map.206 = (bf16[2,640,768]{2,1,0:T(8,128)(2,1)}, f32[16,768]{1,0:T(8,128)}, f32[16,768]{1,0:T(8,128)}, f32[16,768]{1,0:T(8,128)}, f32[16,2048]{1,0:T(8,12...) custom-call(s32[128,8]{1,0:T(8,128)} %copy.25.ids_ref, bf16[128,8]{1,0:T(8,128)(2,1)} %copy.26.gates_ref, ...), custom_call_target="tpu_custom_call" | custom-call | tf_op jit(solution)/shard_map/pallas_call | solution.py:492
  150.9 0.0 copy-start.6
  150.9 0.0 copy-start.5
  150.9 0.0 copy-start.4
  150.9 0.0 copy-start.3
  150.9 0.0 copy-start.2
  150.9 0.0 copy-start.1
  150.9 3.0 %copy.35 = bf16[2,640,768]{2,1,0:T(8,128)(2,1)} copy(bf16[2,640,768]{2,1,0:T(8,128)(2,1)} %get-tuple-element.32) | data formatting | bytes 3932160
  154.0 0.6 copy.36
  154.6 0.6 copy.37
  155.2 0.0 copy-done.4
  155.2 0.6 copy.38
  155.8 0.0 copy-done.3
  155.8 0.7 copy.39
  156.5 0.0 copy-done.2
  156.5 0.7 copy.40
  157.2 0.0 copy-done.1
  157.2 0.7 copy.41
  157.8 0.0 copy-done
  157.8 0.7 copy.42
  (3 shorter events, 0.0 us)
Async XLA Ops:
  150.9 3.1 %copy-start.6 = (f32[16,768]{1,0:T(8,128)S(1)}, f32[16,768]{1,0:T(8,128)}, u32[]{:S(2)}) copy-start(f32[16,768]{1,0:T(8,128)} %get-tuple-element.17) | copy-start | bytes 147460
  150.9 3.7 %copy-start.5 = (f32[16,768]{1,0:T(8,128)S(1)}, f32[16,768]{1,0:T(8,128)}, u32[]{:S(2)}) copy-start(f32[16,768]{1,0:T(8,128)} %get-tuple-element.18) | copy-start | bytes 147460
  150.9 4.3 %copy-start.4 = (f32[16,768]{1,0:T(8,128)S(1)}, f32[16,768]{1,0:T(8,128)}, u32[]{:S(2)}) copy-start(f32[16,768]{1,0:T(8,128)} %get-tuple-element.19) | copy-start | bytes 147460
  150.9 5.0 %copy-start.3 = (f32[16,2048]{1,0:T(8,128)S(1)}, f32[16,2048]{1,0:T(8,128)}, u32[]{:S(2)}) copy-start(f32[16,2048]{1,0:T(8,128)} %get-tuple-element.20) | copy-start | bytes 393220
  150.9 5.6 %copy-start.2 = (f32[16,2048]{1,0:T(8,128)S(1)}, f32[16,2048]{1,0:T(8,128)}, u32[]{:S(2)}) copy-start(f32[16,2048]{1,0:T(8,128)} %get-tuple-element.21) | copy-start | bytes 393220
  150.9 6.2 %copy-start.1 = (f32[16,2048]{1,0:T(8,128)S(1)}, f32[16,2048]{1,0:T(8,128)}, u32[]{:S(2)}) copy-start(f32[16,2048]{1,0:T(8,128)} %get-tuple-element.22) | copy-start | bytes 393220
  150.9 6.9 %copy-start = (bf16[32,2048]{1,0:T(8,128)(2,1)S(1)}, bf16[32,2048]{1,0:T(8,128)(2,1)}, u32[]{:S(2)}) copy-start(bf16[32,2048]{1,0:T(8,128)(2,1)} %get-tuple-element.23) | copy-start | bytes 393220

commit v2 on v1

--- a/solution.py
+++ b/solution.py
@@ -23,11 +23,14 @@
 NY, NH = 4, 2
 D, FF, CAP, CAPD = 2048, 768, 20, 4
 TOK, DEC = 128, 32
-NCH = 4
-CW = D // NCH
+CHUNKS = ((0, 128), (128, 128)) + tuple((at, 256) for at in range(256, 2048, 256))
+NCH = len(CHUNKS)
+NP = 4
+DCH = 4
+CW = D // DCH
 SB = NZ * CAP
 DB = NZ * 2 * CAPD
-PIECES = ((0, 512), (512, 512), (1024, 512), (1536, 1280))
+PIECES = ((0, 512), (512, 768), (1280, 512), (1792, 1024))
 W = D + FF
 
 
@@ -57,9 +60,10 @@
 
 
 def kernel(
-    ids_ref, gates_ref, dids_ref, dgates_ref, fin_ref, fout_ref,
-    cot_hbm, saved_hbm, base_hbm, min_hbm, mout_hbm, sin_hbm, sout_hbm, dh_hbm, res_hbm,
-    hg_hbm, ain_ref, vin_ref, qin_ref, aout_ref, vout_ref, qout_ref, rout_ref,
+    ids_ref, gates_ref, dids_ref, dgates_ref,
+    fin_hbm, fout_hbm, cot_hbm, saved_hbm, base_hbm, min_hbm, mout_hbm, sin_hbm, sout_hbm, dh_hbm, res_hbm,
+    hg_hbm, ain_hbm, vin_hbm, qin_hbm, aout_hbm, vout_hbm, qout_hbm, rout_hbm,
+    fin_ref, fout_ref, ain_ref, vin_ref, qin_ref, aout_ref, vout_ref, qout_ref, rout_ref,
     xa, lms, lmr, dms, dmr, fg, pmat, lr, lg, ob, inc,
     saved, base, mi, mo, si, so, dh, res,
     perm, savedp, lit, lo, tg, ry, ss, sz, rz, rg,
@@ -113,17 +117,22 @@
         cp.start()
         loads[name] = cp
 
+    def chunk(ch):
+        return pl.ds(*CHUNKS[ch])
+
     own_rows = pl.ds(pl.multiple_of(z * TOK, TOK), TOK)
     for ch in range(NCH):
-        load(("cot", ch), ch, cot_hbm.at[:, pl.ds(ch * CW, CW)], xa.at[ch, own_rows])
-    load("saved", 4, saved_hbm, saved)
-    load("base", 5, base_hbm, base)
-    load("dh", 6, dh_hbm, dh)
-    load("mi", 7, min_hbm, mi)
-    load("mo", 8, mout_hbm, mo)
-    load("si", 9, sin_hbm, si)
-    load("so", 10, sout_hbm, so)
-    load("res", 11, res_hbm, res)
+        load(("cot", ch), 10 + ch, cot_hbm.at[:, chunk(ch)], xa.at[own_rows, chunk(ch)])
+    load("fin", 8, fin_hbm, fin_ref)
+    load("fout", 9, fout_hbm, fout_ref)
+    load("saved", 0, saved_hbm, saved)
+    load("base", 1, base_hbm, base)
+    load("dh", 2, dh_hbm, dh)
+    load("mi", 3, min_hbm, mi)
+    load("mo", 4, mout_hbm, mo)
+    load("si", 5, sin_hbm, si)
+    load("so", 6, sout_hbm, so)
+    load("res", 7, res_hbm, res)
 
     barrier = pltpu.get_barrier_semaphore()
     for z2 in zpeers:
@@ -134,72 +143,70 @@
         pl.semaphore_signal(barrier, inc=1, device_id=ydev(y2), device_id_type=MESH)
     pl.semaphore_signal(barrier, inc=1, device_id=hdev, device_id_type=MESH)
 
-    own = pl.ds(grp, 1)
-    fg[own, :, 0:D] = fout_ref[...].astype(BF)[None]
-    fg[own, :, D:W] = fin_ref[...].astype(BF)[None]
-
-    lane = iota((TOK, 128), 1)
-    count = jnp.zeros((TOK, 128), F32)
-    gate = jnp.zeros((TOK, 128), F32)
-    ids = ids_ref[...]
-    gw = gates_ref[...].astype(F32)
-    for k in range(8):
-        hit = ids[:, k : k + 1] == lane
-        count = count + jnp.where(hit, 1.0, 0.0)
-        gate = gate + jnp.where(hit, gw[:, k : k + 1], 0.0)
-    rows, cols = iota((TOK, TOK), 0), iota((TOK, TOK), 1)
-    before = jnp.where(rows < cols, 1.0, 0.0).astype(BF)
-    eye = jnp.where(rows == cols, 1.0, 0.0).astype(BF)
-    cb = count.astype(BF)
-    rank_t = tn(cb, before)
-    count_t = tn(cb, eye)
-    gate_t = tn(gate.astype(BF), eye)
-    row_t = jnp.where(count_t > 0.5, rank_t + (CAP * z).astype(F32), -1.0).astype(BF)
-    gate_t = gate_t.astype(BF)
+    pl.semaphore_wait(barrier, 14)
+
+    def send_tokens(ch):
+        loads[("cot", ch)].wait()
+        for k, z2 in enumerate(zpeers):
+            part = xa.at[own_rows, chunk(ch)]
+            push(part, part, zt_s.at[ch, k], zt_r.at[ch, z], zdev(z2))
+
+    send_tokens(0)
+
+    def tables(ids, gates):
+        n = ids.shape[1]
+        expert = iota((64, n), 0)
+        count = jnp.zeros((64, n), F32)
+        gate = jnp.zeros((64, n), F32)
+        for k in range(8):
+            hit = ids[k : k + 1, :] == expert
+            count = count + jnp.where(hit, 1.0, 0.0)
+            gate = gate + jnp.where(hit, gates[k : k + 1, :], 0.0)
+        before = jnp.where(iota((n, n), 0) < iota((n, n), 1), 1.0, 0.0).astype(BF)
+        return count > 0.5, mm(count.astype(BF), before), gate
+
+    named, rank, gate = tables(ids_ref[...], gates_ref[...].astype(F32))
+    row_t = jnp.where(named, rank + (CAP * z).astype(F32), -1.0).astype(BF)
+    gate_t = gate.astype(BF)
     for z2 in range(NZ):
         lms[z2, 0:16] = row_t[16 * z2 : 16 * z2 + 16]
         lms[z2, 16:32] = gate_t[16 * z2 : 16 * z2 + 16]
 
-    lane = iota((DEC, 128), 1)
-    count = jnp.zeros((DEC, 128), F32)
-    gate = jnp.zeros((DEC, 128), F32)
-    ids = dids_ref[...]
-    gw = dgates_ref[...]
-    for k in range(8):
-        hit = ids[:, k : k + 1] == lane
-        count = count + jnp.where(hit, 1.0, 0.0)
-        gate = gate + jnp.where(hit, gw[:, k : k + 1], 0.0)
-    rows, cols = iota((DEC, DEC), 0), iota((DEC, DEC), 1)
-    before = jnp.where((cols < rows) & ((cols >> 4) == (rows >> 4)), 1.0, 0.0).astype(BF)
-    rank = mm(before, count.astype(BF))
-    high = gate.astype(BF)
-    dms[0:32] = jnp.where(count > 0.5, rank, -1.0).astype(BF)
-    dms[32:64] = high
-    dms[64:96] = (gate - high.astype(F32)).astype(BF)
-
-    pl.semaphore_wait(barrier, 14)
-
-    push(fg.at[own], fg.at[own], fz_s.at[0], fz_r.at[0], hdev)
     for k, z2 in enumerate(zpeers):
         push(lms.at[z2], lmr.at[z], lm_s.at[k], lm_r.at[z], zdev(z2))
-
-    def send_tokens(ch):
-        loads[("cot", ch)].wait()
-        for k, z2 in enumerate(zpeers):
-            push(xa.at[ch, own_rows], xa.at[ch, own_rows], zt_s.at[ch, k], zt_r.at[ch, z], zdev(z2))
-
-    send_tokens(0)
-    send_tokens(1)
+    lmr[pl.ds(z, 1)] = lms[pl.ds(z, 1)]
+
+    own = pl.ds(grp, 1)
+    loads["fin"].wait()
+    loads["fout"].wait()
+    fg[own, :, 0:D] = fout_ref[...].astype(BF)[None]
+    fg[own, :, D:W] = fin_ref[...].astype(BF)[None]
+
+    push(fg.at[own], fg.at[own], fz_s.at[0], fz_r.at[0], hdev)
+
+    flip = jnp.where(iota((64, 128), 0) == iota((64, 128), 1), 1.0, 0.0).astype(BF)
+    for step in range(2):
+        named, rank, gate = tables(dids_ref[step], dgates_ref[step])
+        high = gate.astype(BF)
+        low = (gate - high.astype(F32)).astype(BF)
+        at = step * 16
+        dms[at : at + 16] = tn(jnp.where(named, rank, -1.0).astype(BF), flip).astype(BF)
+        dms[32 + at : 48 + at] = tn(high, flip).astype(BF)
+        dms[64 + at : 80 + at] = tn(low, flip).astype(BF)
+
     for k, z2 in enumerate(zpeers):
         push(dms, dmr.at[z], dm_s.at[k], dm_r.at[z], zdev(z2))
-    lmr[pl.ds(z, 1)] = lms[pl.ds(z, 1)]
     dmr[pl.ds(z, 1)] = dms[...][None]
 
-    pair = pl.ds(pl.multiple_of(y * NH, NH), NH)
-    other = pl.ds(y * NH + (1 - h), 1)
-    arrived(fg.at[other], fz_s.at[0], fz_r.at[0], hdev)
-    for k, y2 in enumerate(ypeers):
-        push(fg.at[pair], fg.at[pair], fy_s.at[k], fy_r.at[y], ydev(y2))
+    def permutation(source):
+        n = source.shape[0]
+        return jnp.where(iota((n, n), 1) == source, 1.0, 0.0).astype(BF)
+
+    p_id = iota((NQ * SB, 1), 0)
+    blk = (p_id * 3277) >> 16
+    off = p_id - blk * CAP
+    perm[0] = permutation((blk & 3) * (NQ * CAP) + (blk >> 2) * CAP + off)
+    perm[1] = permutation((blk & 7) * SB + (blk >> 3) * CAP + off)
 
     for z2 in zpeers:
         arrived(lmr.at[z2], lm_s.at[0], lm_r.at[z2], zdev(z2))
@@ -218,29 +225,31 @@
 
     def expand(ch, q2):
         w = pmat[pl.ds(q2 * 2, 2)].reshape(2 * SB, NZ * TOK)
-        return mm(w, xa[ch]).astype(BF).reshape(2, SB, CW)
+        return mm(w, xa[:, chunk(ch)]).astype(BF).reshape(2, SB, CHUNKS[ch][1])
 
     def build_send(ch):
         for z2 in zpeers:
-            dst = xa.at[ch, pl.ds(pl.multiple_of(z2 * TOK, TOK), TOK)]
+            dst = xa.at[pl.ds(pl.multiple_of(z2 * TOK, TOK), TOK), chunk(ch)]
             arrived(dst, zt_s.at[ch, 0], zt_r.at[ch, z2], zdev(z2))
+        if ch == 0:
+            send_tokens(1)
         if ch + 2 < NCH:
             send_tokens(ch + 2)
+        cc = chunk(ch)
         for k, q2 in enumerate(qpeers):
-            ob[ch, k] = expand(ch, q2)
-            push(ob.at[ch, k], inc.at[ch, :, q], x_s.at[ch, k], x_r.at[ch, q], qdev(q2))
-        inc[ch, :, pl.ds(q, 1)] = expand(ch, q)[:, None]
+            ob[k, :, :, cc] = expand(ch, q2)
+            push(ob.at[k, :, :, cc], inc.at[:, q, :, cc], x_s.at[ch, k], x_r.at[ch, q], qdev(q2))
+        inc[:, pl.ds(q, 1), :, cc] = expand(ch, q)[:, None]
 
     build_send(0)
 
-    def permutation(n, source):
-        return jnp.where(iota((n, n), 1) == source, 1.0, 0.0).astype(BF)
-
-    p_id = iota((NQ * SB, NQ * SB), 0)
-    blk = (p_id * 3277) >> 16
-    off = p_id - blk * CAP
-    perm[0] = permutation(NQ * SB, (blk & 3) * (NQ * CAP) + (blk >> 2) * CAP + off)
-    perm[1] = permutation(NQ * SB, (blk & 7) * SB + (blk >> 3) * CAP + off)
+    pair = pl.ds(pl.multiple_of(y * NH, NH), NH)
+    other = pl.ds(y * NH + (1 - h), 1)
+    arrived(fg.at[other], fz_s.at[0], fz_r.at[0], hdev)
+    for k, y2 in enumerate(ypeers):
+        push(fg.at[pair], fg.at[pair], fy_s.at[k], fy_r.at[y], ydev(y2))
+
+    build_send(1)
     loads["saved"].wait()
 
     def permute_saved(e, carry):
@@ -248,6 +257,7 @@
         return carry
 
     lax.fori_loop(0, 2, permute_saved, 0)
+    build_send(2)
 
     for y2 in ypeers:
         blocks = pl.ds(pl.multiple_of(y2 * NH, NH), NH)
@@ -264,22 +274,21 @@
         return carry
 
     lax.fori_loop(0, 2, low_in, 0)
-
-    build_send(1)
+    build_send(3)
 
     def consume(ch):
         for q2 in qpeers:
-            arrived(inc.at[ch, :, q2], x_s.at[ch, 0], x_r.at[ch, q2], qdev(q2))
-        cc = pl.ds(ch * CW, CW)
-        weights = fg[:, :, cc].reshape(128, CW)
+            arrived(inc.at[:, q2, :, chunk(ch)], x_s.at[ch, 0], x_r.at[ch, q2], qdev(q2))
+        cc, cw = chunk(ch), CHUNKS[ch][1]
+        weights = fg[:, :, cc].reshape(128, cw)
 
         def one(e, acc):
-            rows = inc[ch, e].reshape(NQ * SB, CW)
+            rows = inc[e, :, :, cc].reshape(NQ * SB, cw)
             lo[e] += nt(rows, weights)
             return acc + mm(lit[e], rows)
 
-        term = lax.fori_loop(0, 2, one, jnp.zeros((128, CW), F32))
-        tg[:, :, cc] = term.astype(BF).reshape(8, 16, CW)
+        term = lax.fori_loop(0, 2, one, jnp.zeros((128, cw), F32))
+        tg[:, :, cc] = term.astype(BF).reshape(8, 16, cw)
 
     def cols_of(p):
         return pl.ds(PIECES[p][0], PIECES[p][1])
@@ -312,11 +321,12 @@
             return share * (ss[h, :, at] + rz[:, at].astype(F32))
 
         start = PIECES[p][0]
-        at = pl.ds(start, CW)
-        new, first, second = adam_update(fout_ref[:, at], mo[:, at], so[:, at], grad(start, CW))
+        width = min(PIECES[p][1], D - start)
+        at = pl.ds(start, width)
+        new, first, second = adam_update(fout_ref[:, at], mo[:, at], so[:, at], grad(start, width))
         aout_ref[:, at], vout_ref[:, at], qout_ref[:, at] = new, first, second
         rg[own, :, at] = new.astype(BF)[None]
-        if p == NCH - 1:
+        if p == NP - 1:
             new, first, second = adam_update(fin_ref[...], mi[...], si[...], grad(D, FF))
             ain_ref[...], vin_ref[...], qin_ref[...] = new, first, second
             rg[own, :, D:W] = new.astype(BF)[None]
@@ -334,24 +344,30 @@
             blocks = pl.ds(pl.multiple_of(y2 * NH, NH), NH)
             arrived(rg.at[blocks, :, cc], ay_s.at[p, 0], ay_r.at[p, y2], ydev(y2))
 
-    n = iota((512, 512), 0)
+    consume(0)
+
+    n = iota((512, 1), 0)
     source = ((n >> 2) & 1) * 256 + (n >> 8) * 128 + ((n >> 3) & 3) * 32 + ((n >> 5) & 7) * 4 + (n & 3)
-    dperm[...] = permutation(512, source)
+    dperm[...] = permutation(source)
     loads["dh"].wait()
     dhp[...] = mm(dperm[...], dh[...]).astype(BF).reshape(2, 256, FF)
+
+    build_send(4)
+    consume(1)
+    consume(2)
+    rs_start(0)
+
     loads["base"].wait()
 
     def base_product(k, carry):
-        e, ch = k // NCH, k % NCH
+        e, ch = k // DCH, k % DCH
         at = pl.ds(pl.multiple_of(ch * CW, CW), CW)
         dbase[e, :, at] = mm(dhp[e], base[e, :, at])
         return carry
 
-    lax.fori_loop(0, 2 * NCH, base_product, 0)
-
-    consume(0)
-    rs_start(0)
-    build_send(2)
+    lax.fori_loop(0, 2 * DCH, base_product, 0)
+    build_send(5)
+    consume(3)
 
     for z2 in zpeers:
         arrived(dmr.at[z2], dm_s.at[0], dm_r.at[z2], zdev(z2))
@@ -368,15 +384,20 @@
     for name in ("mi", "mo", "si", "so", "res"):
         loads[name].wait()
 
-    consume(1)
+    rs_mid(0)
+    build_send(6)
+    consume(4)
+    build_send(7)
+    consume(5)
     rs_start(1)
-    rs_mid(0)
-    build_send(3)
-    consume(2)
+    rs_fin(0)
+    build_send(8)
+    consume(6)
+    ag_mid(0)
+    consume(7)
     rs_start(2)
     rs_mid(1)
-    rs_fin(0)
-    consume(3)
+    consume(8)
 
     def term_in(e, acc):
         low = jnp.where(lane_mask(NQ * SB, e), lo[e], 0.0)
@@ -388,17 +409,16 @@
     rs_start(3)
     rs_mid(2)
     rs_fin(1)
-    ag_mid(0)
 
     def hidden(e):
         hgacc[...] = delta_scale * mm(lo[e].astype(BF), fg[:, :, D:W].reshape(128, FF))
 
         def part(ch, carry):
             at = pl.ds(pl.multiple_of(ch * CW, CW), CW)
-            hgacc[...] += nt(inc[ch, e].reshape(NQ * SB, CW), base[e, :, at])
+            hgacc[...] += nt(inc[e, :, :, at].reshape(NQ * SB, CW), base[e, :, at])
             return carry
 
-        lax.fori_loop(0, NCH, part, 0)
+        lax.fori_loop(0, DCH, part, 0)
         hgp[...] = hgacc[...].astype(BF)
         hgn[e] = mm(perm[1], hgp[...]).astype(BF)
         cp = pltpu.make_async_copy(hgn.at[e], hg_hbm.at[e], out_sem.at[e])
@@ -411,6 +431,13 @@
     ag_mid(1)
     rs_fin(3)
     ag_mid(2)
+    stores = []
+    for k, (src, dst) in enumerate((
+        (ain_ref, ain_hbm), (vin_ref, vin_hbm), (qin_ref, qin_hbm),
+        (aout_ref, aout_hbm), (vout_ref, vout_hbm), (qout_ref, qout_hbm),
+    )):
+        stores.append(pltpu.make_async_copy(src, dst, out_sem.at[2 + k]))
+        stores[-1].start()
     out1 = hidden(1)
     ag_mid(3)
     ag_fin(0)
@@ -422,7 +449,7 @@
     for e in range(2):
         low = nt(dhp[e], rg[:, :, D:W].reshape(128, FF))
         low_d.append(jnp.where(lane_mask(256, e), low, 0.0).astype(BF))
-    for ch in range(NCH):
+    for ch in range(DCH):
         at = pl.ds(ch * CW, CW)
         weights = rg[:, :, at].reshape(128, CW)
         for e in range(2):
@@ -431,7 +458,7 @@
         for k, q2 in enumerate(qpeers):
             push(pd.at[ch, q2], rd.at[ch, q], dx_s.at[ch, k], dx_r.at[ch, q], qdev(q2))
         rd[ch, pl.ds(q, 1)] = pd[ch, pl.ds(q, 1)]
-    for ch in range(NCH):
+    for ch in range(DCH):
         for q2 in qpeers:
             arrived(rd.at[ch, q2], dx_s.at[ch, 0], dx_r.at[ch, q2], qdev(q2))
         rows = rd[ch].reshape(512, CW)
@@ -440,7 +467,7 @@
         for k, z2 in enumerate(zpeers):
             push(pz.at[ch, z2], rzd.at[ch, z], dz_s.at[ch, k], dz_r.at[ch, z], zdev(z2))
         rzd[ch, pl.ds(z, 1)] = pz[ch, pl.ds(z, 1)]
-    for ch in range(NCH):
+    for ch in range(DCH):
         at = pl.ds(ch * CW, CW)
         for z2 in zpeers:
             arrived(rzd.at[ch, z2], dz_s.at[ch, 0], dz_r.at[ch, z2], zdev(z2))
@@ -449,10 +476,27 @@
             total = total + rzd[ch, z2].astype(F32)
         rout_ref[:, at] = total.astype(BF)
 
+    stores.append(pltpu.make_async_copy(rout_ref, rout_hbm, out_sem.at[8]))
+    stores[-1].start()
     out0.wait()
     out1.wait()
+    for cp in stores:
+        cp.wait()
     for cp in sends:
         cp.wait_send()
+
+
+def hand_over(*refs):
+    made, results, held, sem = refs[:8], refs[8:16], refs[16:24], refs[24]
+    arriving = [pltpu.make_async_copy(made[k], held[k], sem.at[0, k]) for k in range(8)]
+    leaving = [pltpu.make_async_copy(held[k], results[k], sem.at[1, k]) for k in range(8)]
+    for cp in arriving:
+        cp.start()
+    for k in (1, 2, 3, 4, 5, 6, 7, 0):
+        arriving[k].wait()
+        leaving[k].start()
+    for cp in leaving:
+        cp.wait()
 
 
 def on_device(
@@ -467,11 +511,14 @@
     S = pltpu.SemaphoreType.DMA
     n = NQ * SB
     scratch = [
-        V((NCH, NZ * TOK, CW), BF),
+        V((16, FF), F32), V((16, D), F32),
+        V((16, FF), F32), V((16, FF), F32), V((16, FF), F32),
+        V((16, D), F32), V((16, D), F32), V((16, D), F32), V((DEC, D), BF),
+        V((NZ * TOK, D), BF),
         V((NZ, 32, TOK), BF), V((NZ, 32, TOK), BF), V((96, 128), BF), V((NZ, 96, 128), BF),
         V((8, 16, W), BF),
         V((2 * NQ, SB, NZ * TOK), BF), V((16, NZ * TOK), F32), V((16, NZ * TOK), F32),
-        V((NCH, 7, 2, SB, CW), BF), V((NCH, 2, NQ, SB, CW), BF),
+        V((7, 2, SB, D), BF), V((2, NQ, SB, D), BF),
         V((2, n, FF), BF), V((2, FF, D), BF),
         V((16, FF), F32), V((16, D), F32), V((16, FF), F32), V((16, D), F32),
         V((512, FF), BF), V((DEC, D), BF),
@@ -481,13 +528,13 @@
         V((n, FF), F32), V((n, FF), BF), V((2, n, FF), BF),
         V((512, 512), BF), V((2, 256, FF), BF), V((2, 256, D), F32),
         V((2, 128, 512), BF), V((3, 128, 128), BF),
-        V((NCH, NQ, 2, DB, CW), BF), V((NCH, NQ, 2, DB, CW), BF),
-        V((NCH, NZ, DEC, CW), BF), V((NCH, NZ, DEC, CW), BF),
-        S((12,)), S((2,)), S((NCH, 3)), S((NCH, NZ)), S((3,)), S((NZ,)), S((3,)), S((NZ,)),
+        V((DCH, NQ, 2, DB, CW), BF), V((DCH, NQ, 2, DB, CW), BF),
+        V((DCH, NZ, DEC, CW), BF), V((DCH, NZ, DEC, CW), BF),
+        S((10 + NCH,)), S((9,)), S((NCH, 3)), S((NCH, NZ)), S((3,)), S((NZ,)), S((3,)), S((NZ,)),
         S((1,)), S((1,)), S((3,)), S((NY,)),
-        S((NCH, 7)), S((NCH, NQ)), S((NCH, 3)), S((NCH, NY)), S((NCH,)), S((NCH,)),
-        S((NCH,)), S((NCH,)), S((NCH, 3)), S((NCH, NY)),
-        S((NCH, 7)), S((NCH, NQ)), S((NCH, 3)), S((NCH, NZ)),
+        S((NCH, 7)), S((NCH, NQ)), S((NP, 3)), S((NP, NY)), S((NP,)), S((NP,)),
+        S((NP,)), S((NP,)), S((NP, 3)), S((NP, NY)),
+        S((DCH, 7)), S((DCH, NQ)), S((DCH, 3)), S((DCH, NZ)),
     ]
     outs = pl.pallas_call(
         kernel,
@@ -497,24 +544,31 @@
             sds((16, D), F32), sds((16, D), F32), sds((16, D), F32),
             sds((DEC, D), BF),
         ),
-        in_specs=[vm] * 6 + [hbm] * 9,
-        out_specs=(hbm,) + (vm,) * 7,
+        in_specs=[vm] * 4 + [hbm] * 11,
+        out_specs=(hbm,) * 8,
         scratch_shapes=scratch,
         compiler_params=pltpu.CompilerParams(
             collective_id=0, has_side_effects=True, vmem_limit_bytes=60 * 1024 * 1024
         ),
     )(
-        expert_ids, gate_weights, decode_ids.reshape(DEC, 8), decode_gates.reshape(DEC, 8),
+        expert_ids.T, gate_weights.T, decode_ids.transpose(0, 2, 1), decode_gates.transpose(0, 2, 1),
         flat(factor_in), flat(factor_out),
         cotangent, saved_hidden, base_down, flat(mean_in), flat(mean_out), flat(square_in), flat(square_out),
         decode_hidden.reshape(512, FF), residual_in.reshape(DEC, D),
     )
     hg, ain, vin, qin, aout, vout, qout, rout = outs
     wide = lambda a: a.reshape(2, 8, a.shape[-1])
-    return (
+    made = (
         hg, wide(ain), wide(vin), wide(qin), wide(aout), wide(vout), wide(qout),
         rout.reshape(2, DEC // 2, D),
     )
+    return pl.pallas_call(
+        hand_over,
+        out_shape=tuple(sds(a.shape, a.dtype) for a in made),
+        in_specs=[hbm] * 8,
+        out_specs=(hbm,) * 8,
+        scratch_shapes=[V(a.shape, a.dtype) for a in made] + [S((2, 8))],
+    )(*made)
 
 
 def solution(mesh):

time: 159 us -> 143 us (0.90)
  local copies, waits for them, and re-layouts: 13.1 us -> 0 us
  Pallas kernels: 145 us -> 141 us
    unnamed x26 -> x0, local copies, waits for them, and re-layouts: 13.1 us -> none
    pallas_call x1, Pallas kernels: 145 us -> 138 us  [on_device(): pl.pallas_call(kernel, out_shape=(sds((2, n, FF), BF), sds((16, FF), F32)...]
    pallas_call x0 -> x1, Pallas kernels: none -> 3.14 us  [on_device(): pl.pallas_call(hand_over, out_shape=tuple((sds(a.shape, a.dtype) for a in...]
where the time goes in v2:
time: 143 us; the launch traced here: 142 us
  Pallas kernels  141 us (99%)
    pallas_call x1, Pallas kernels, on_device(): pl.pallas_call(kernel, out_shape=(sds((2, n, FF), BF), sds((16, FF), F32)...  138 us
    pallas_call x1, Pallas kernels, on_device(): pl.pallas_call(hand_over, out_shape=tuple((sds(a.shape, a.dtype) for a in...  3.14 us

profile of v2, /device:TPU:1, one launch (start us, length us, event | category | flops | bytes accessed | tf_op | source)
XLA Modules:
  0.0 141.5 jit_solution(14977686615508925533)
XLA Ops:
  0.6 137.6 %shard_map.206 = (bf16[2,640,768]{2,1,0:T(8,128)(2,1)}, f32[16,768]{1,0:T(8,128)}, f32[16,768]{1,0:T(8,128)}, f32[16,768]{1,0:T(8,128)}, f32[16,2048]{1,0:T(8,12...) custom-call(s32[8,128]{1,0:T(8,128)} %bitcast.36, bf16[8,128]{1,0:T(8,128)(2,1)} %bitcast.37, ...), custom_call_target="tpu_custom_call" | custom-call | tf_op jit(solution)/shard_map/pallas_call | solution.py:539
  138.2 3.1 %shard_map.207 = (bf16[2,640,768]{2,1,0:T(8,128)(2,1)}, f32[2,8,768]{2,1,0:T(8,128)}, f32[2,8,768]{2,1,0:T(8,128)}, f32[2,8,768]{2,1,0:T(8,128)}, f32[2,8,2048]{...) custom-call(bf16[2,640,768]{2,1,0:T(8,128)(2,1)} %get-tuple-element.16.refs_0_, ...), custom_call_target="tpu_custom_call" | custom-call | tf_op jit(solution)/shard_map/pallas_call | solution.py:565

commit v3 on v2

v3 whole, which is shorter than its diff:
```python
import functools

import jax
import jax.numpy as jnp
from jax import lax
from jax.experimental import pallas as pl
from jax.experimental.pallas import tpu as pltpu
from jax.sharding import PartitionSpec as P

delta_scale = 0.5
learn_rate = 0.005
beta_first = 0.9
beta_second = 0.999
adam_count = 20.0
adam_eps = 1e-08

BF = jnp.bfloat16
F32 = jnp.float32
MESH = pl.DeviceIdType.MESH

NZ, NX, NC = 4, 4, 2
NQ = NX * NC
NY, NH = 4, 2
D, FF, CAP, CAPD = 2048, 768, 20, 4
TOK, DEC = 128, 32
CHUNKS = tuple((at, 256) for at in range(0, 2048, 256))
NCH = len(CHUNKS)
UNITS = (
    (0, 0), (1, 0), (0, 1), (1, 1), (0, 2), (0, 3), (1, 2), (0, 4), (0, 5), (1, 3), (0, 6), (0, 7),
    (1, 4), (1, 5), (1, 6), (1, 7),
)
LAG = 3
NP = 3
DCH = 4
CW = D // DCH
SB = NZ * CAP
DB = NZ * 2 * CAPD
PIECES = ((0, 1280), (1280, 512), (1792, 1024))
W = D + FF


def nt(a, b):
    return lax.dot_general(a, b, (((1,), (1,)), ((), ())), preferred_element_type=F32)


def tn(a, b):
    return lax.dot_general(a, b, (((0,), (0,)), ((), ())), preferred_element_type=F32)


def mm(a, b):
    return jnp.dot(a, b, preferred_element_type=F32)


def iota(shape, axis):
    return lax.broadcasted_iota(jnp.int32, shape, axis)


def adam_update(parameter, moment_one, moment_two, gradient):
    first_new = beta_first * moment_one + (1.0 - beta_first) * gradient
    second_new = beta_second * moment_two + (1.0 - beta_second) * gradient * gradient
    fix_first = 1.0 - beta_first**adam_count
    fix_second = 1.0 - beta_second**adam_count
    update = first_new / fix_first / (jnp.sqrt(second_new / fix_second) + adam_eps)
    return (parameter - learn_rate * update, first_new, second_new)


def kernel(
    ids_ref, gates_ref, dids_ref, dgates_ref,
    fin_hbm, fout_hbm, cot_hbm, saved_hbm, base_hbm, min_hbm, mout_hbm, sin_hbm, sout_hbm, dh_hbm, res_hbm,
    hg_hbm, ain_hbm, vin_hbm, qin_hbm, aout_hbm, vout_hbm, qout_hbm, rout_hbm,
    fin_ref, fout_ref, ain_ref, vin_ref, qin_ref, aout_ref, vout_ref, qout_ref, rout_ref,
    xa, lms, lmr, dms, dmr, fg, pmat, lr, lg, ob, inc,
    saved, base, mi, mo, si, so, dh, res,
    perm, savedp, lit, lo, tg, ry, ss, sz, rz, rh, ah, ar, rg,
    hgacc, hgp, hgn, dperm, dhp, dbase, amat, drs, pd, rd, pacc, pz, rzd,
    in_sem, out_sem, zt_s, zt_r, lm_s, lm_r, dm_s, dm_r, fz_s, fz_r, fy_s, fy_r,
    x_s, x_r, ry_s, ry_r, rz_s, rz_r, az_s, az_r, ay_s, ay_r, dx_s, dx_r, dz_s, dz_r,
):
    dp = lax.axis_index("dp")
    grp = lax.axis_index("group")
    z = dp // NQ
    q = dp % NQ
    x = q // NC
    c = q % NC
    y = grp // NH
    h = grp % NH

    def zdev(z2):
        return (z2 * NQ + q, grp)

    def qdev(q2):
        return (z * NQ + q2, grp)

    def ydev(y2):
        return (dp, y2 * NH + h)

    hdev = (dp, y * NH + (1 - h))
    zpeers = [(z + k) % NZ for k in (1, 2, 3)]
    ypeers = [(y + k) % NY for k in (2, 1, 3)]
    qpeers = [
        ((x + dx) % NX) * NC + (c + dc) % NC
        for dx, dc in ((2, 0), (2, 1), (1, 0), (3, 1), (1, 1), (3, 0), (0, 1))
    ]
    barrier = pltpu.get_barrier_semaphore()
    for z2 in zpeers:
        pl.semaphore_signal(barrier, inc=1, device_id=zdev(z2), device_id_type=MESH)
    for q2 in qpeers:
        pl.semaphore_signal(barrier, inc=1, device_id=qdev(q2), device_id_type=MESH)
    for y2 in ypeers:
        pl.semaphore_signal(barrier, inc=1, device_id=ydev(y2), device_id_type=MESH)
    pl.semaphore_signal(barrier, inc=1, device_id=hdev, device_id_type=MESH)

    sends = []

    def push(src, dst, ssem, rsem, dev):
        cp = pltpu.make_async_remote_copy(
            src_ref=src, dst_ref=dst, send_sem=ssem, recv_sem=rsem, device_id=dev, device_id_type=MESH
        )
        cp.start()
        sends.append(cp)

    def arrived(dst, ssem, rsem, dev):
        pltpu.make_async_remote_copy(
            src_ref=dst, dst_ref=dst, send_sem=ssem, recv_sem=rsem, device_id=dev, device_id_type=MESH
        ).wait_recv()

    loads = {}

    def load(name, k, src, dst):
        cp = pltpu.make_async_copy(src, dst, in_sem.at[k])
        cp.start()
        loads[name] = cp

    def chunk(ch):
        return pl.ds(*CHUNKS[ch])

    own_rows = pl.ds(pl.multiple_of(z * TOK, TOK), TOK)
    for ch in range(NCH):
        load(("cot", ch), 10 + ch, cot_hbm.at[:, chunk(ch)], xa.at[own_rows, chunk(ch)])
    load("fin", 8, fin_hbm, fin_ref)
    load("fout", 9, fout_hbm, fout_ref)
    load("saved", 0, saved_hbm, saved)
    load("base", 1, base_hbm, base)
    load("dh", 2, dh_hbm, dh)
    load("mi", 3, min_hbm, mi)
    load("mo", 4, mout_hbm, mo)
    load("si", 5, sin_hbm, si)
    load("so", 6, sout_hbm, so)
    load("res", 7, res_hbm, res)

    def tables(ids, gates):
        n = ids.shape[1]
        expert = iota((64, n), 0)
        count = jnp.zeros((64, n), F32)
        gate = jnp.zeros((64, n), F32)
        for k in range(8):
            hit = ids[k : k + 1, :] == expert
            count = count + jnp.where(hit, 1.0, 0.0)
            gate = gate + jnp.where(hit, gates[k : k + 1, :], 0.0)
        before = jnp.where(iota((n, n), 0) < iota((n, n), 1), 1.0, 0.0).astype(BF)
        return count > 0.5, mm(count.astype(BF), before), gate

    named, rank, gate = tables(ids_ref[...], gates_ref[...].astype(F32))
    row_t = jnp.where(named, rank + (CAP * z).astype(F32), -1.0).astype(BF)
    gate_t = gate.astype(BF)
    for z2 in range(NZ):
        lms[z2, 0:16] = row_t[16 * z2 : 16 * z2 + 16]
        lms[z2, 16:32] = gate_t[16 * z2 : 16 * z2 + 16]

    pl.semaphore_wait(barrier, 14)

    leaving = []
    left = set()

    def send_tokens(ch):
        loads[("cot", ch)].wait()
        for k, z2 in enumerate(zpeers):
            part = xa.at[own_rows, chunk(ch)]
            leaving.append((ch, len(sends)))
            push(part, part, zt_s.at[ch, k], zt_r.at[ch, z], zdev(z2))

    send_tokens(0)
    for k, z2 in enumerate(zpeers):
        push(lms.at[z2], lmr.at[z], lm_s.at[k], lm_r.at[z], zdev(z2))
    lmr[pl.ds(z, 1)] = lms[pl.ds(z, 1)]

    own = pl.ds(grp, 1)
    loads["fin"].wait()
    loads["fout"].wait()
    fg[own, :, 0:D] = fout_ref[...].astype(BF)[None]
    fg[own, :, D:W] = fin_ref[...].astype(BF)[None]

    push(fg.at[own], fg.at[own], fz_s.at[0], fz_r.at[0], hdev)

    flip = jnp.where(iota((64, 128), 0) == iota((64, 128), 1), 1.0, 0.0).astype(BF)
    for step in range(2):
        named, rank, gate = tables(dids_ref[step], dgates_ref[step])
        high = gate.astype(BF)
        low = (gate - high.astype(F32)).astype(BF)
        at = step * 16
        dms[at : at + 16] = tn(jnp.where(named, rank, -1.0).astype(BF), flip).astype(BF)
        dms[32 + at : 48 + at] = tn(high, flip).astype(BF)
        dms[64 + at : 80 + at] = tn(low, flip).astype(BF)

    for k, z2 in enumerate(zpeers):
        push(dms, dmr.at[z], dm_s.at[k], dm_r.at[z], zdev(z2))
    dmr[pl.ds(z, 1)] = dms[...][None]

    def permutation(source):
        n = source.shape[0]
        return jnp.where(iota((n, n), 1) == source, 1.0, 0.0).astype(BF)

    p_id = iota((NQ * SB, 1), 0)
    blk = (p_id * 3277) >> 16
    off = p_id - blk * CAP
    perm[0] = permutation((blk & 3) * (NQ * CAP) + (blk >> 2) * CAP + off)
    perm[1] = permutation((blk & 7) * SB + (blk >> 3) * CAP + off)

    for z2 in zpeers:
        arrived(lmr.at[z2], lm_s.at[0], lm_r.at[z2], zdev(z2))
    for z2 in range(NZ):
        lr[:, z2 * TOK : (z2 + 1) * TOK] = lmr[z2, 0:16].astype(F32)
        lg[:, z2 * TOK : (z2 + 1) * TOK] = lmr[z2, 16:32].astype(F32)
    slot = iota((SB, NZ * TOK), 0).astype(F32)

    for e in range(2):

        def build_p(q2, carry):
            row = lr[pl.ds(q2 * 2 + e, 1), :]
            val = lg[pl.ds(q2 * 2 + e, 1), :]
            pmat[e, q2] = jnp.where(slot == row, val, 0.0).astype(BF)
            return carry

        lax.fori_loop(0, NQ, build_p, 0)

    def tokens(ch):
        for of, k in leaving:
            if of == ch:
                sends[k].wait_send()
                left.add(k)
        if ch + 1 < NCH:
            send_tokens(ch + 1)
        for z2 in zpeers:
            dst = xa.at[pl.ds(pl.multiple_of(z2 * TOK, TOK), TOK), chunk(ch)]
            arrived(dst, zt_s.at[ch, 0], zt_r.at[ch, z2], zdev(z2))

    def build_send(e, ch):
        cc, at = chunk(ch), e * NCH + ch
        made = mm(pmat[e].reshape(NQ * SB, NZ * TOK), xa[:, cc])
        ob[e, :, :, cc] = made.astype(BF).reshape(NQ, SB, CHUNKS[ch][1])
        for k, q2 in enumerate(qpeers):
            push(ob.at[e, q2, :, cc], inc.at[e, q, :, cc], x_s.at[at, k], x_r.at[at, q], qdev(q2))
        inc[e, pl.ds(q, 1), :, cc] = ob[e, pl.ds(q, 1), :, cc]

    def lane_mask(n, e):
        return ((iota((n, 128), 1) >> 3) & 1) == e

    def own_ranks(low, e):
        n = low.shape[0]
        return low.T.reshape(8, 2, 8, n)[:, e].reshape(64, n).astype(BF)

    def consume(e, ch):
        cc, cw, at = chunk(ch), CHUNKS[ch][1], e * NCH + ch
        for q2 in qpeers:
            arrived(inc.at[e, q2, :, cc], x_s.at[at, 0], x_r.at[at, q2], qdev(q2))
        rows = inc[e, :, :, cc].reshape(NQ * SB, cw)
        lo[e] += nt(rows, fg[:, :, cc].reshape(128, cw))
        tg[e, :, :, cc] = mm(lit[e], rows).astype(BF).reshape(NY, 16, cw)

    def term_in(e):
        low = jnp.where(lane_mask(NQ * SB, e), lo[e], 0.0)
        lo[e] = low
        tg[e, :, :, D:W] = mm(own_ranks(low, e), savedp[e]).astype(BF).reshape(NY, 16, FF)

    def cols_of(p):
        return pl.ds(PIECES[p][0], PIECES[p][1])

    def half(p):
        return pl.ds(PIECES[p][0] // 2, PIECES[p][1] // 2)

    def pack(a):
        n = a.shape[1] // 2
        return jnp.concatenate([a[:, :n], a[:, n:]], axis=0).astype(BF)

    def unpack(a):
        a = a.astype(F32)
        return jnp.concatenate([a[:8], a[8:]], axis=1)

    def rs_start(e, p):
        cc, at = cols_of(p), e * NP + p
        for k, y2 in enumerate(ypeers):
            push(tg.at[e, y2, :, cc], ry.at[e, y, :, cc], ry_s.at[at, k], ry_r.at[at, y], ydev(y2))
        ry[e, pl.ds(y, 1), :, cc] = tg[e, pl.ds(y, 1), :, cc]

    def rs_mid(e, p):
        cc, at = cols_of(p), e * NP + p
        for y2 in ypeers:
            arrived(ry.at[e, y2, :, cc], ry_s.at[at, 0], ry_r.at[at, y2], ydev(y2))
        total = ry[e, 0, :, cc].astype(F32)
        for y2 in range(1, NY):
            total = total + ry[e, y2, :, cc].astype(F32)
        ss[e, :, :, cc] = total.reshape(NH, 8, PIECES[p][1])
        sz[e, :, half(p)] = pack(ss[e, pl.ds(1 - h, 1), :, cc].reshape(8, PIECES[p][1]))
        push(sz.at[e, :, half(p)], rz.at[e, :, half(p)], rz_s.at[at], rz_r.at[at], hdev)

    def rs_fin(e, p):
        cc, at = cols_of(p), e * NP + p
        arrived(rz.at[e, :, half(p)], rz_s.at[at], rz_r.at[at], hdev)
        share = delta_scale / (NY * NH)
        er = pl.ds(e * 8, 8)
        start, width = PIECES[p]
        own_sum = ss[e, pl.ds(h, 1), :, cc].reshape(8, width)
        grad = share * (own_sum + unpack(rz[e, :, half(p)]))
        n = min(width, D - start)
        part = pl.ds(start, n)
        new, first, second = adam_update(fout_ref[er, part], mo[er, part], so[er, part], grad[:, :n])
        aout_ref[er, part], vout_ref[er, part], qout_ref[er, part] = new, first, second
        if p == NP - 1:
            new_in, first, second = adam_update(fin_ref[er, :], mi[er, :], si[er, :], grad[:, n:])
            ain_ref[er, :], vin_ref[er, :], qin_ref[er, :] = new_in, first, second
            new = jnp.concatenate([new, new_in], axis=1)
        rh[e, pl.ds(h, 1), :, cc] = new[None]
        ah[e, :, half(p)] = pack(new)
        push(ah.at[e, :, half(p)], ar.at[e, :, half(p)], az_s.at[at], az_r.at[at], hdev)

    def ag_mid(e, p):
        cc, at = cols_of(p), e * NP + p
        arrived(ar.at[e, :, half(p)], az_s.at[at], az_r.at[at], hdev)
        rh[e, pl.ds(1 - h, 1), :, cc] = unpack(ar[e, :, half(p)])[None]
        rg[e, pl.ds(y, 1), :, cc] = rh[e, :, :, cc].reshape(1, 16, PIECES[p][1]).astype(BF)
        for k, y2 in enumerate(ypeers):
            push(rg.at[e, y, :, cc], rg.at[e, y, :, cc], ay_s.at[at, k], ay_r.at[at, y], ydev(y2))

    def ag_fin(e, p):
        cc, at = cols_of(p), e * NP + p
        for y2 in ypeers:
            arrived(rg.at[e, y2, :, cc], ay_s.at[at, 0], ay_r.at[at, y2], ydev(y2))

    def hidden(e):
        hgacc[...] = delta_scale * mm(lo[e].astype(BF), fg[:, :, D:W].reshape(128, FF))

        def part(ch, carry):
            at = pl.ds(pl.multiple_of(ch * CW, CW), CW)
            hgacc[...] += nt(inc[e, :, :, at].reshape(NQ * SB, CW), base[e, :, at])
            return carry

        lax.fori_loop(0, DCH, part, 0)
        hgp[...] = hgacc[...].astype(BF)
        hgn[e] = mm(perm[1], hgp[...]).astype(BF)
        cp = pltpu.make_async_copy(hgn.at[e], hg_hbm.at[e], out_sem.at[e])
        cp.start()
        return cp

    def decode_send(e):
        low = nt(dhp[e], rg[e, :, :, D:W].reshape(64, FF)).astype(BF)
        for ch in range(DCH):
            part, at = pl.ds(ch * CW, CW), e * DCH + ch
            made = dbase[e, :, part] + delta_scale * mm(low, rg[e, :, :, part].reshape(64, CW))
            pd[e, ch] = made.astype(BF).reshape(NQ, DB, CW)
            for k, q2 in enumerate(qpeers):
                push(pd.at[e, ch, q2], rd.at[e, ch, q], dx_s.at[at, k], dx_r.at[at, q], qdev(q2))
            rd[e, ch, pl.ds(q, 1)] = pd[e, ch, pl.ds(q, 1)]

    def gated(e, ch):
        at = e * DCH + ch
        for q2 in qpeers:
            arrived(rd.at[e, ch, q2], dx_s.at[at, 0], dx_r.at[at, q2], qdev(q2))
        rows = rd[e, ch].reshape(256, CW)
        return mm(amat[0, :, e * 256 : e * 256 + 256], rows) + mm(amat[1, :, e * 256 : e * 256 + 256], rows)

    def share_factors():
        pair = pl.ds(pl.multiple_of(y * NH, NH), NH)
        other = pl.ds(y * NH + (1 - h), 1)
        arrived(fg.at[other], fz_s.at[0], fz_r.at[0], hdev)
        for k, y2 in enumerate(ypeers):
            push(fg.at[pair], fg.at[pair], fy_s.at[k], fy_r.at[y], ydev(y2))

    def order_saved():
        loads["saved"].wait()

        def permute_saved(e, carry):
            savedp[e] = mm(perm[0], saved[e]).astype(BF)
            return carry

        lax.fori_loop(0, 2, permute_saved, 0)

    def low_inputs():
        for y2 in ypeers:
            blocks = pl.ds(pl.multiple_of(y2 * NH, NH), NH)
            arrived(fg.at[blocks], fy_s.at[0], fy_r.at[y2], ydev(y2))

        for e in range(2):
            lit[e] = own_ranks(nt(savedp[e], fg[:, :, D:W].reshape(128, FF)), e)
            lo[e] = jnp.zeros((NQ * SB, 128), F32)

    def order_decode():
        n = iota((512, 1), 0)
        source = ((n >> 2) & 1) * 256 + (n >> 8) * 128 + ((n >> 3) & 3) * 32 + ((n >> 5) & 7) * 4 + (n & 3)
        dperm[...] = permutation(source)
        loads["dh"].wait()
        dhp[...] = mm(dperm[...], dh[...]).astype(BF).reshape(2, 256, FF)

    def gate_matrix():
        for z2 in zpeers:
            arrived(dmr.at[z2], dm_s.at[0], dm_r.at[z2], zdev(z2))
        for z2 in range(NZ):
            for k in range(3):
                drs[k, z2 * DEC : (z2 + 1) * DEC] = dmr[z2, k * DEC : (k + 1) * DEC]
        j = iota((128, 512), 1)
        spread = jnp.where(iota((128, 512), 0) == z * 16 + ((j >> 5) & 7) * 2 + (j >> 8), 1.0, 0.0).astype(BF)
        i = iota((128, 512), 0)
        ok = (mm(drs[0], spread) == (j & 3).astype(F32)) & ((i >> 5) == ((j >> 3) & 3)) & (((i >> 4) & 1) == ((j >> 2) & 1))
        amat[0] = jnp.where(ok, mm(drs[1], spread), 0.0).astype(BF)
        amat[1] = jnp.where(ok, mm(drs[2], spread), 0.0).astype(BF)

        for name in ("mi", "mo", "si", "so", "res"):
            loads[name].wait()

    def base_products():
        loads["base"].wait()

        def base_product(k, carry):
            e, ch = k // DCH, k % DCH
            at = pl.ds(pl.multiple_of(ch * CW, CW), CW)
            dbase[e, :, at] = mm(dhp[e], base[e, :, at])
            return carry

        lax.fori_loop(0, 2 * DCH, base_product, 0)

    done_with = {}

    def hide():
        done_with["out0"] = hidden(0)

    before = {
        1: [share_factors], 3: [order_saved], 5: [low_inputs], 6: [order_decode], 8: [gate_matrix], 9: [base_products],
    }
    after = {
        7: [(rs_start, 0, 0)],
        9: [(rs_mid, 0, 0)],
        10: [(rs_start, 0, 1), (rs_fin, 0, 0)],
        11: [(term_in, 0), (rs_start, 0, 2), (rs_mid, 0, 1), (ag_mid, 0, 0)],
        12: [(rs_start, 1, 0), (rs_mid, 0, 2), (rs_fin, 0, 1), (hide,)],
        13: [(rs_fin, 0, 2), (ag_mid, 0, 1), (rs_mid, 1, 0)],
        14: [(rs_start, 1, 1), (ag_mid, 0, 2), (rs_fin, 1, 0)],
        15: [(term_in, 1), (rs_start, 1, 2), (rs_mid, 1, 1), (ag_mid, 1, 0)],
    }
    used = 0
    for k, (e, ch) in enumerate(UNITS):
        for task in before.get(k, ()):
            task()
        if e == 0:
            tokens(ch)
        build_send(e, ch)
        while k >= 5 and used <= k - LAG or k == len(UNITS) - 1 and used < len(UNITS):
            consume(*UNITS[used])
            for task in after.get(used, ()):
                task[0](*task[1:])
            used += 1

    for p in range(NP):
        ag_fin(0, p)
    decode_send(0)
    rs_mid(1, 2)
    rs_fin(1, 1)
    rs_fin(1, 2)
    ag_mid(1, 1)
    stores = []
    for k, (src, dst) in enumerate((
        (ain_ref, ain_hbm), (vin_ref, vin_hbm), (qin_ref, qin_hbm),
        (aout_ref, aout_hbm), (vout_ref, vout_hbm), (qout_ref, qout_hbm),
    )):
        stores.append(pltpu.make_async_copy(src, dst, out_sem.at[2 + k]))
        stores[-1].start()
    ag_mid(1, 2)
    for p in range(NP):
        ag_fin(1, p)
    decode_send(1)
    for ch in range(DCH):
        pacc[ch] = gated(0, ch)
    out0 = done_with["out0"]
    out1 = hidden(1)

    for ch in range(DCH):
        part = pacc[ch] + gated(1, ch)
        pz[ch] = part.astype(BF).reshape(NZ, DEC, CW)
        for k, z2 in enumerate(zpeers):
            push(pz.at[ch, z2], rzd.at[ch, z], dz_s.at[ch, k], dz_r.at[ch, z], zdev(z2))
        rzd[ch, pl.ds(z, 1)] = pz[ch, pl.ds(z, 1)]
    for ch in range(DCH):
        at = pl.ds(ch * CW, CW)
        for z2 in zpeers:
            arrived(rzd.at[ch, z2], dz_s.at[ch, 0], dz_r.at[ch, z2], zdev(z2))
        total = res[:, at].astype(F32)
        for z2 in range(NZ):
            total = total + rzd[ch, z2].astype(F32)
        rout_ref[:, at] = total.astype(BF)

    stores.append(pltpu.make_async_copy(rout_ref, rout_hbm, out_sem.at[8]))
    stores[-1].start()
    out0.wait()
    out1.wait()
    for cp in stores:
        cp.wait()
    for k, cp in enumerate(sends):
        if k not in left:
            cp.wait_send()


def hand_over(*refs):
    made, results, held, sem = refs[:8], refs[8:16], refs[16:24], refs[24]
    arriving = [pltpu.make_async_copy(made[k], held[k], sem.at[0, k]) for k in range(8)]
    leaving = [pltpu.make_async_copy(held[k], results[k], sem.at[1, k]) for k in range(8)]
    for cp in arriving:
        cp.start()
    for k in (1, 2, 3, 4, 5, 6, 7, 0):
        arriving[k].wait()
        leaving[k].start()
    for cp in leaving:
        cp.wait()


def on_device(
    cotangent, gate_weights, expert_ids, saved_hidden, base_down, factor_in, factor_out,
    mean_in, mean_out, square_in, square_out, decode_hidden, decode_ids, decode_gates, residual_in,
):
    flat = lambda a: a.reshape(16, a.shape[-1])
    vm = pl.BlockSpec(memory_space=pltpu.VMEM)
    hbm = pl.BlockSpec(memory_space=pl.ANY)
    sds = jax.ShapeDtypeStruct
    V = pltpu.VMEM
    S = pltpu.SemaphoreType.DMA
    n = NQ * SB
    scratch = [
        V((16, FF), F32), V((16, D), F32),
        V((16, FF), F32), V((16, FF), F32), V((16, FF), F32),
        V((16, D), F32), V((16, D), F32), V((16, D), F32), V((DEC, D), BF),
        V((NZ * TOK, D), BF),
        V((NZ, 32, TOK), BF), V((NZ, 32, TOK), BF), V((96, 128), BF), V((NZ, 96, 128), BF),
        V((8, 16, W), BF),
        V((2, NQ, SB, NZ * TOK), BF), V((16, NZ * TOK), F32), V((16, NZ * TOK), F32),
        V((2, NQ, SB, D), BF), V((2, NQ, SB, D), BF),
        V((2, n, FF), BF), V((2, FF, D), BF),
        V((16, FF), F32), V((16, D), F32), V((16, FF), F32), V((16, D), F32),
        V((512, FF), BF), V((DEC, D), BF),
        V((2, n, n), BF), V((2, n, FF), BF), V((2, 64, n), BF), V((2, n, 128), F32),
        V((2, NY, 16, W), BF), V((2, NY, 16, W), BF), V((2, NH, 8, W), F32),
        V((2, 16, W // 2), BF), V((2, 16, W // 2), BF), V((2, NH, 8, W), F32),
        V((2, 16, W // 2), BF), V((2, 16, W // 2), BF), V((2, NY, 16, W), BF),
        V((n, FF), F32), V((n, FF), BF), V((2, n, FF), BF),
        V((512, 512), BF), V((2, 256, FF), BF), V((2, 256, D), F32),
        V((2, 128, 512), BF), V((3, 128, 128), BF),
        V((2, DCH, NQ, DB, CW), BF), V((2, DCH, NQ, DB, CW), BF), V((DCH, 128, CW), F32),
        V((DCH, NZ, DEC, CW), BF), V((DCH, NZ, DEC, CW), BF),
        S((10 + NCH,)), S((9,)), S((NCH, 3)), S((NCH, NZ)), S((3,)), S((NZ,)), S((3,)), S((NZ,)),
        S((1,)), S((1,)), S((3,)), S((NY,)),
        S((2 * NCH, 7)), S((2 * NCH, NQ)), S((2 * NP, 3)), S((2 * NP, NY)), S((2 * NP,)), S((2 * NP,)),
        S((2 * NP,)), S((2 * NP,)), S((2 * NP, 3)), S((2 * NP, NY)),
        S((2 * DCH, 7)), S((2 * DCH, NQ)), S((DCH, 3)), S((DCH, NZ)),
    ]
    outs = pl.pallas_call(
        kernel,
        out_shape=(
            sds((2, n, FF), BF),
            sds((16, FF), F32), sds((16, FF), F32), sds((16, FF), F32),
            sds((16, D), F32), sds((16, D), F32), sds((16, D), F32),
            sds((DEC, D), BF),
        ),
        in_specs=[vm] * 4 + [hbm] * 11,
        out_specs=(hbm,) * 8,
        scratch_shapes=scratch,
        compiler_params=pltpu.CompilerParams(
            collective_id=0, has_side_effects=True, vmem_limit_bytes=60 * 1024 * 1024
        ),
    )(
        expert_ids.T, gate_weights.T, decode_ids.transpose(0, 2, 1), decode_gates.transpose(0, 2, 1),
        flat(factor_in), flat(factor_out),
        cotangent, saved_hidden, base_down, flat(mean_in), flat(mean_out), flat(square_in), flat(square_out),
        decode_hidden.reshape(512, FF), residual_in.reshape(DEC, D),
    )
    hg, ain, vin, qin, aout, vout, qout, rout = outs
    wide = lambda a: a.reshape(2, 8, a.shape[-1])
    made = (
        hg, wide(ain), wide(vin), wide(qin), wide(aout), wide(vout), wide(qout),
        rout.reshape(2, DEC // 2, D),
    )
    return pl.pallas_call(
        hand_over,
        out_shape=tuple(sds(a.shape, a.dtype) for a in made),
        in_specs=[hbm] * 8,
        out_specs=(hbm,) * 8,
        scratch_shapes=[V(a.shape, a.dtype) for a in made] + [S((2, 8))],
    )(*made)


def solution(mesh):
    in_specs = (
        P(("dp", "group"), None),
        P(("dp", "group"), None),
        P(("dp", "group"), None),
        P("dp", "group", None),
        P("dp", None, None),
        P("dp", "group", None),
        P("dp", "group", None),
        P("dp", "group", None),
        P("dp", "group", None),
        P("dp", "group", None),
        P("dp", "group", None),
        P(None, "dp", "group", None),
        P(None, ("dp", "group"), None),
        P(None, ("dp", "group"), None),
        P(None, ("dp", "group"), None),
    )
    out_specs = (
        P("dp", "group", None),
        P("dp", "group", None),
        P("dp", "group", None),
        P("dp", "group", None),
        P("dp", "group", None),
        P("dp", "group", None),
        P("dp", "group", None),
        P(None, ("dp", "group"), None),
    )
    return jax.shard_map(
        on_device, mesh=mesh, in_specs=in_specs, out_specs=out_specs, check_vma=False
    )
```

time: 143 us -> 141 us (0.986); the launches traced: 142 us -> 141 us
  no operation moved by 1% of the time
where the time goes in v3:
time: 141 us
  Pallas kernels  140 us (99%)
    pallas_call x1, Pallas kernels, on_device(): pl.pallas_call(kernel, out_shape=(sds((2, n, FF), BF), sds((16, FF), F32)...  137 us
    pallas_call x1, Pallas kernels, on_device(): pl.pallas_call(hand_over, out_shape=tuple((sds(a.shape, a.dtype) for a in...  3.14 us

profile of v3, /device:TPU:1, one launch (start us, length us, event | category | flops | bytes accessed | tf_op | source)
XLA Modules:
  0.0 141.1 jit_solution(13932578437890639185)
XLA Ops:
  0.6 137.1 %shard_map.206 = (bf16[2,640,768]{2,1,0:T(8,128)(2,1)}, f32[16,768]{1,0:T(8,128)}, f32[16,768]{1,0:T(8,128)}, f32[16,768]{1,0:T(8,128)}, f32[16,2048]{1,0:T(8,12...) custom-call(s32[8,128]{1,0:T(8,128)} %bitcast.36, bf16[8,128]{1,0:T(8,128)(2,1)} %bitcast.37, ...), custom_call_target="tpu_custom_call" | custom-call | tf_op jit(solution)/shard_map/pallas_call | solution.py:561
  137.8 3.1 %shard_map.207 = (bf16[2,640,768]{2,1,0:T(8,128)(2,1)}, f32[2,8,768]{2,1,0:T(8,128)}, f32[2,8,768]{2,1,0:T(8,128)}, f32[2,8,768]{2,1,0:T(8,128)}, f32[2,8,2048]{...) custom-call(bf16[2,640,768]{2,1,0:T(8,128)(2,1)} %get-tuple-element.16.refs_0_, ...), custom_call_target="tpu_custom_call" | custom-call | tf_op jit(solution)/shard_map/pallas_call | solution.py:587
